TPU v7x, 512 devices: a whole 4x8x8 slice. The times are simulated.
512 devices in a mesh: wide: 128 (over z, y, core), narrow: 4 (over x).
Axes of the slice: x: 4, y: 8, z: 8, core: 2. Of those that a mesh axis runs over, the one named last changes fastest.
Arguments:
- statistics: float32 [128, 2, 512, 512], P(None, None, 'wide', 'narrow'), as said below
- gradients: bfloat16 [128, 512, 512], P(None, 'wide', 'narrow'), may hold values from -6 to 6
- assign: int32 [128, 2], replicated, may hold values from 0 to 127, as said below
- counts: int32 [128], replicated, may hold values from 0 to 2, as said below
Outputs:
- inverse_roots: float32 [128, 2, 512, 512], P(None, None, 'wide', 'narrow')
- root_diagonals: float32 [128, 2, 512], P(None, None, 'wide')
- directions: bfloat16 [128, 2, 512, 512], P('wide')
Inputs may be any that keep to these rules, and one draw needn't show every extreme that they name: `assign`: for worker w the first counts[w] entries are the blocks it roots; over all workers these name every block of 0 to 127 exactly once. Entries at slots from counts[w] on are arbitrary block numbers. The counts sum to 128; some worker roots 2 blocks and some none. `statistics`: every factor is symmetric and positive definite.
All inputs are finite; a program needn't handle non-finite values.
Results may differ from a plain program's by a relative error of at most 0.0065.
Values may be sent and summed in bfloat16 or wider, within the bound.
A program may use at most 64 MiB of HBM per device.

v0:
```python
import jax
import jax.numpy as jnp
from jax import lax
from jax.sharding import PartitionSpec as P

BLOCK = 512
ITERS = 2


def partner_2(block, axis, stride):
    count = lax.axis_size(axis)
    route = []
    for low in range(count):
        high = low | 1 << stride
        if high != low and high < count:
            route += [(low, high), (high, low)]
    return lax.ppermute(block, axis, route)


def batched_product(first, second):
    return jnp.einsum(
        "kij,kjl->kil",
        first,
        second,
        precision=lax.Precision.HIGHEST,
        preferred_element_type=jnp.float32,
    )


def inverse_fourth_root(factors):
    identity = jnp.eye(factors.shape[-1], dtype=jnp.float32)
    frobenius = jnp.sqrt(jnp.sum(factors * factors, axis=(1, 2), keepdims=True))
    scaling = 2.5 / frobenius
    current = scaling * factors
    iterate = current
    for iteration in range(ITERS):
        step_matrix = 0.25 * (5.0 * identity - current)
        if iteration == 0:
            iterate = jnp.sqrt(jnp.sqrt(scaling)) * step_matrix
        else:
            iterate = batched_product(iterate, step_matrix)
        if iteration + 1 < ITERS:
            square = batched_product(step_matrix, step_matrix)
            current = batched_product(batched_product(square, square), current)
    return iterate


def apply_pair(left_low, right_low, gradient):
    half_product = jnp.dot(left_low, gradient, preferred_element_type=jnp.float32).astype(
        jnp.bfloat16
    )
    return jnp.dot(half_product, right_low, preferred_element_type=jnp.float32).astype(jnp.bfloat16)


def return_rows(own_root, assign, counts, block_total, narrow_count):
    wide_count = assign.shape[0]
    shard_rows = BLOCK // wide_count
    shard_cols = BLOCK // narrow_count
    on_diagonal = jnp.eye(BLOCK, dtype=bool)
    off_root = jnp.where(on_diagonal, jnp.zeros_like(own_root), own_root)
    diagonal = jnp.diagonal(own_root).reshape(wide_count, shard_rows)
    outgoing = off_root.reshape(1, wide_count, shard_rows, narrow_count, shard_cols)
    diag_out = jnp.broadcast_to(
        diagonal[None, :, :, None, None], (1, wide_count, shard_rows, narrow_count, 1)
    )
    incoming, incoming_diag = (
        lax.all_to_all(
            lax.all_to_all(outgoing, "wide", split_axis=1, concat_axis=0, tiled=True),
            "narrow",
            split_axis=3,
            concat_axis=0,
            tiled=True,
        ),
        lax.all_to_all(
            lax.all_to_all(diag_out, "wide", split_axis=1, concat_axis=0, tiled=True),
            "narrow",
            split_axis=3,
            concat_axis=0,
            tiled=True,
        ),
    )
    incoming = incoming.reshape(narrow_count, wide_count, shard_rows, shard_cols)
    incoming_diag = incoming_diag.reshape(narrow_count, wide_count, shard_rows)
    device_slot = jnp.arange(narrow_count, dtype=jnp.int32) // 2
    occupied = device_slot[:, None] < counts[None, :]
    listed_grid = jnp.repeat(assign.T, 2, axis=0)
    target = jnp.where(occupied, listed_grid, block_total)
    side_grid = jnp.broadcast_to(
        (jnp.arange(narrow_count, dtype=jnp.int32) % 2)[:, None], (narrow_count, wide_count)
    )
    blank_roots = jnp.zeros((block_total, 2, shard_rows, shard_cols), jnp.float32)
    blank_diag = jnp.zeros((block_total, 2, shard_rows), jnp.float32)
    placed_roots = blank_roots.at[target, side_grid].set(incoming, mode="drop")
    placed_diag = blank_diag.at[target, side_grid].set(incoming_diag, mode="drop")
    return (placed_roots, placed_diag)


def per_device(statistics, gradients, assign, counts):
    wide_count, slot_count = assign.shape
    narrow_count = lax.axis_size("narrow")
    wide_index = lax.axis_index("wide")
    narrow_index = lax.axis_index("narrow")
    slot_index = narrow_index // 2
    side_index = narrow_index % 2
    occupied = slot_index < counts[wide_index]
    shard_rows, shard_cols = (statistics.shape[2], statistics.shape[3])
    listed = jnp.repeat(assign, 2, axis=1).reshape(wide_count * narrow_count)
    grad_packed = gradients[listed].reshape(wide_count, narrow_count, 1, shard_rows, shard_cols)
    gradient = lax.all_to_all(
        lax.all_to_all(grad_packed, "wide", split_axis=0, concat_axis=3, tiled=True),
        "narrow",
        split_axis=1,
        concat_axis=4,
        tiled=True,
    )[0, 0, 0]
    blank_root = jnp.zeros((BLOCK, BLOCK), jnp.float32)
    blank_direction = jnp.zeros((BLOCK, BLOCK), jnp.bfloat16)
    sides = jnp.arange(wide_count * narrow_count, dtype=jnp.int32) % 2
    packed = statistics[listed, sides].reshape(wide_count, narrow_count, 1, shard_rows, shard_cols)
    factor = lax.all_to_all(
        lax.all_to_all(packed, "wide", split_axis=0, concat_axis=3, tiled=True),
        "narrow",
        split_axis=1,
        concat_axis=4,
        tiled=True,
    )[0, 0]

    def rooted(single):
        return inverse_fourth_root(single)[0]

    def unrooted(single):
        return blank_root

    own_root = lax.cond(occupied, rooted, unrooted, factor)
    own_low = own_root.astype(jnp.bfloat16)
    partner = partner_2(own_low, "narrow", 0)
    is_left = side_index == 0
    left_low = jnp.where(is_left, own_low, partner)
    right_low = jnp.where(is_left, partner, own_low)

    def applied(operands):
        return apply_pair(operands[0], operands[1], operands[2])

    def unapplied(operands):
        return blank_direction

    direction = lax.cond(occupied, applied, unapplied, (left_low, right_low, gradient))
    inverse_roots, root_diagonals = return_rows(
        own_root, assign, counts, statistics.shape[0], narrow_count
    )
    own_half = lax.dynamic_index_in_dim(
        direction.reshape(2, BLOCK // 2, BLOCK), side_index, 0, keepdims=False
    )
    gathered = lax.all_gather(own_half[None, None], "narrow", axis=1, tiled=True)
    directions = gathered.reshape(1, slot_count, BLOCK, BLOCK)
    return (inverse_roots, root_diagonals, directions)


def solution(mesh):
    return jax.shard_map(
        per_device,
        mesh=mesh,
        in_specs=(P(None, None, "wide", "narrow"), P(None, "wide", "narrow"), P(), P()),
        out_specs=(
            P(None, None, "wide", "narrow"),
            P(None, None, "wide"),
            P("wide", None, None, None),
        ),
        check_vma=False,
    )
```

profile of v0, /device:TPU:1, one launch (start us, length us, event | category | flops | bytes accessed | tf_op | source)
XLA Modules:
  0.0 257.6 jit_solution(15962819453897888703)
XLA Ops:
  8.4 2.5 gather_fusion
  10.9 1.2 copy.65
  12.2 18.6 %all-to-all-start = ((f32[128,4,1,4,128]{4,1,3,2,0:T(4,128)}), f32[128,4,1,4,128]{4,1,3,2,0:T(4,128)S(1)}, u32[]{:S(2)}, u32[]{:S(2)}) async-start(f32[128,4,1,4,128]{4,1,3,2,0:T(4,128)} %copy.65), calls=%async_computation | async-start | bytes 2097152 | tf_op jit(solution)/shard_map/all_to_all | solution.py:121
  30.8 2.1 gather_fusion.2
  33.9 27.8 %all-to-all-done = f32[128,4,1,4,128]{4,1,3,2,0:T(4,128)S(1)} async-done(((f32[128,4,1,4,128]{4,1,3,2,0:T(4,128)}), f32[128,4,1,4,128]{4,1,3,2,0:T(4,128)S(1)}, u32[]{:S(2)}, u32[]{:S(2)}) %all-to-all-start) | async-done | bytes 1048608 | tf_op jit(solution)/shard_map/all_to_all | solution.py:121
  61.6 6.5 %all-to-all-start.6 = ((bf16[128,4,1,4,128]{4,1,3,2,0:T(4,128)(2,1)}), bf16[128,4,1,4,128]{4,1,3,2,0:T(4,128)(2,1)S(1)}, u32[]{:S(2)}, u32[]{:S(2)}) async-start(bf16[128,4,1,4,128]{4,1,3,2,0:T(4,128)(2,1)} %copy.71), calls=%async_computation.6 | async-start | bytes 1048576 | tf_op jit(solution)/shard_map/all_to_all | solution.py:110
  69.2 19.5 %all-to-all-done.6 = bf16[128,4,1,4,128]{4,1,3,2,0:T(4,128)(2,1)S(1)} async-done(((bf16[128,4,1,4,128]{4,1,3,2,0:T(4,128)(2,1)}), bf16[128,4,1,4,128]{4,1,3,2,0:T(4,128)(2,1)S(1)}, u32[]{:S(2)}, u32[]{:S(2)}) %all-to-all-start.6) | async-done | bytes 524320 | tf_op jit(solution)/shard_map/all_to_all | solution.py:110
  88.7 4.0 %all-to-all-start.1 = ((f32[1,4,1,512,128]{4,3,2,0,1:T(8,128)}), f32[1,4,1,512,128]{4,3,2,0,1:T(8,128)S(1)}, u32[]{:S(2)}, u32[]{:S(2)}) async-start(f32[1,4,1,512,128]{4,3,2,0,1:T(8,128)} %copy.66), calls=%async_computation.1 | async-start | bytes 2097152 | tf_op jit(solution)/shard_map/all_to_all | solution.py:120
  93.6 14.4 %all-to-all-done.1 = f32[1,4,1,512,128]{4,3,2,0,1:T(8,128)S(1)} async-done(((f32[1,4,1,512,128]{4,3,2,0,1:T(8,128)}), f32[1,4,1,512,128]{4,3,2,0,1:T(8,128)S(1)}, u32[]{:S(2)}, u32[]{:S(2)}) %all-to-all-start.1) | async-done | bytes 1048608 | tf_op jit(solution)/shard_map/all_to_all | solution.py:120
  108.0 3.5 %all-to-all-start.7 = ((bf16[1,4,1,512,128]{4,3,2,0,1:T(8,128)(2,1)}), bf16[1,4,1,512,128]{4,3,2,0,1:T(8,128)(2,1)S(1)}, u32[]{:S(2)}, u32[]{:S(2)}) async-start(bf16[1,4,1,512,128]{4,3,2,0,1:T(8,128)(2,1)} %copy.72), calls=%async_computation.7 | async-start | bytes 1048576 | tf_op jit(solution)/shard_map/all_to_all | solution.py:109
  113.4 15.0 %conditional.2 = (f32[512,512]{1,0:T(8,128)S(1)}, bf16[512,512]{1,0:T(8,128)(2,1)}) conditional(s32[]{:T(128)} %convert_element_type.19, () %tuple.29, f32[1,1,1,512,4,128]{5,3,4,2,1,0:T(8,128)S(1)} %bitcast.63), branch_computations={%region_0.1_spmd, %region_1.3_spmd} | conditional | flops 6446645248 | bytes 20447308 | solution.py:134
  115.8 3.6 %fusion.4 = f32[512,512]{1,0:T(8,128)S(1)} fusion(f32[1,512,512]{1,2,0:T(8,128)S(1)} %fusion.6), kind=kOutput, calls=%fused_computation.10 | convolution fusion | flops 1610612736 | bytes 2097152 | tf_op jit(solution)/shard_map/cond/branch_1_fun/kij,kjl->kil/dot_general | solution.py:21
  119.4 1.8 fusion.30
  121.2 1.9 fusion
  123.1 1.3 copy.75
  124.5 3.9 %fusion.29 = (bf16[512,512]{1,0:T(8,128)(2,1)}, f32[512,512]{1,0:T(8,128)S(1)}) fusion(f32[512,512]{1,0:T(8,128)S(1)} %fusion, f32[512,512]{1,0:T(8,128)} %copy.75, f32[]{:T(128)S(6)} %mul.86), kind=kOutput, calls=%fused_computation.57 | convolution fusion | flops 1611923456 | bytes 3670020 | tf_op jit(solution)/shard_map/cond/branch_1_fun/kij,kjl->kil/dot_general | solution.py:21
  128.4 4.5 %gather_fusion.1 = f32[512]{0:T(512)S(1)} fusion(f32[512,512]{1,0:T(8,128)S(1)} %get-tuple-element.44, s32[512]{0:T(512)S(1)} %bitcast.60), kind=kCustom, calls=%fused_computation.1 | custom fusion | bytes 8192 | tf_op jit(solution)/shard_map/jit(diagonal)/cond/branch_0_fun/gather | solution.py:61
  133.8 6.1 %all-to-all-start.4 = ((f32[1,128,4,4,1]{2,3,4,0,1:T(4,128)}), f32[1,128,4,4,1]{2,3,4,0,1:T(4,128)S(1)}, u32[]{:S(2)}, u32[]{:S(2)}) async-start(f32[1,128,4,4,1]{2,3,4,0,1:T(4,128)} %broadcast_in_dim.62), calls=%async_computation.4 | async-start | bytes 524288 | tf_op jit(solution)/shard_map/all_to_all | solution.py:75
  140.1 1.3 reshape.354
  141.4 14.0 %all-to-all-done.4 = f32[1,128,4,4,1]{2,3,4,0,1:T(4,128)S(1)} async-done(((f32[1,128,4,4,1]{2,3,4,0,1:T(4,128)}), f32[1,128,4,4,1]{2,3,4,0,1:T(4,128)S(1)}, u32[]{:S(2)}, u32[]{:S(2)}) %all-to-all-start.4) | async-done | bytes 8224 | tf_op jit(solution)/shard_map/all_to_all | solution.py:75
  155.3 5.6 %all-to-all-start.2 = ((f32[1,128,4,4,128]{4,3,2,0,1:T(4,128)}), f32[1,128,4,4,128]{4,3,2,0,1:T(4,128)S(1)}, u32[]{:S(2)}, u32[]{:S(2)}) async-start(f32[1,128,4,4,128]{4,3,2,0,1:T(4,128)} %reshape.354), calls=%async_computation.2 | async-start | bytes 2097152 | tf_op jit(solution)/shard_map/all_to_all | solution.py:68
  160.9 3.6 %collective-permute-start = (bf16[512,512]{1,0:T(8,128)(2,1)}, bf16[512,512]{1,0:T(8,128)(2,1)S(1)}, u32[]{:S(2)}, u32[]{:S(2)}) collective-permute-start(bf16[512,512]{1,0:T(8,128)(2,1)} %get-tuple-element.45), channel_id=1, source_target_pairs={{0,1},{1,0},{2,3},{3,2},{4,5},{5,4},{6,7},{7,6},{8,9},{9,8},{10,11... | collective-permute-start | bytes 1572872 | tf_op jit(solution)/shard_map/ppermute | solution.py:17
  164.6 11.4 %collective-permute-done = bf16[512,512]{1,0:T(8,128)(2,1)S(1)} collective-permute-done((bf16[512,512]{1,0:T(8,128)(2,1)}, bf16[512,512]{1,0:T(8,128)(2,1)S(1)}, u32[]{:S(2)}, u32[]{:S(2)}) %collective-permute-start) | collective-permute-done | bytes 524320 | tf_op jit(solution)/shard_map/ppermute | solution.py:17
  176.0 2.2 conditional.3
  176.4 1.8 convolution_convert_fusion
  179.6 12.3 %all-to-all-done.2 = f32[1,128,4,4,128]{4,3,2,0,1:T(4,128)S(1)} async-done(((f32[1,128,4,4,128]{4,3,2,0,1:T(4,128)}), f32[1,128,4,4,128]{4,3,2,0,1:T(4,128)S(1)}, u32[]{:S(2)}, u32[]{:S(2)}) %all-to-all-start.2) | async-done | bytes 1048608 | tf_op jit(solution)/shard_map/all_to_all | solution.py:68
  191.9 4.5 %all-to-all-start.5 = ((f32[128,1,4,4,1]{0,2,4,1,3:T(4,128)}), f32[128,1,4,4,1]{0,2,4,1,3:T(4,128)S(1)}, u32[]{:S(2)}, u32[]{:S(2)}) async-start(f32[128,1,4,4,1]{0,2,4,1,3:T(4,128)} %copy.68), calls=%async_computation.5 | async-start | bytes 16384 | tf_op jit(solution)/shard_map/all_to_all | solution.py:74
  196.4 1.2 copy.67
  197.6 3.0 %all-to-all-done.5 = f32[128,1,4,4,1]{0,2,4,1,3:T(4,128)S(1)} async-done(((f32[128,1,4,4,1]{0,2,4,1,3:T(4,128)}), f32[128,1,4,4,1]{0,2,4,1,3:T(4,128)S(1)}, u32[]{:S(2)}, u32[]{:S(2)}) %all-to-all-start.5) | async-done | bytes 8224 | tf_op jit(solution)/shard_map/all_to_all | solution.py:74
  200.6 3.5 %all-to-all-start.3 = ((f32[128,1,4,4,128]{4,2,0,1,3:T(4,128)}), f32[128,1,4,4,128]{4,2,0,1,3:T(4,128)S(1)}, u32[]{:S(2)}, u32[]{:S(2)}) async-start(f32[128,1,4,4,128]{4,2,0,1,3:T(4,128)} %copy.67), calls=%async_computation.3 | async-start | bytes 2097152 | tf_op jit(solution)/shard_map/all_to_all | solution.py:67
  205.1 23.8 %scatter_fusion.1 = f32[128,2,4]{2,1,0:T(2,128)S(1)} fusion(f32[128,2,4]{2,1,0:T(2,128)S(1)} %broadcast_in_dim.60, s32[512]{0:T(512)S(1)} %fusion.24, f32[512,4]{1,0:T(8,128)S(1)} %copy.69), kind=kCustom, calls=%fused_computation.4 | custom fusion | bytes 28672 | tf_op jit(solution)/shard_map/scatter | solution.py:94
  229.7 19.9 %scatter_fusion = f32[128,2,4,128]{3,2,1,0:T(4,128)S(1)} fusion(f32[128,2,4,128]{3,2,1,0:T(4,128)S(1)} %broadcast_in_dim.32, s32[512]{0:T(512)S(1)} %fusion.24, f32[512,4,128]{2,1,0:T(4,128)S(1)} %bitcast.65), kind=kCustom, calls=%fused_computation.3 | custom fusion | bytes 3149824 | tf_op jit(solution)/shard_map/scatter | solution.py:93
  (47 shorter events, 12.5 us)
Async XLA Ops:
  7.2 1.3 copy-start
  12.2 18.6 %copy-start.2 = (bf16[128,4,128]{2,1,0:T(4,128)(2,1)S(1)}, bf16[128,4,128]{2,1,0:T(4,128)(2,1)}, u32[]{:S(2)}) copy-start(bf16[128,4,128]{2,1,0:T(4,128)(2,1)} %param.9) | copy-start | bytes 393220
  12.2 49.5 %all-to-all-start = ((f32[128,4,1,4,128]{4,1,3,2,0:T(4,128)}), f32[128,4,1,4,128]{4,1,3,2,0:T(4,128)S(1)}, u32[]{:S(2)}, u32[]{:S(2)}) async-start(f32[128,4,1,4,128]{4,1,3,2,0:T(4,128)} %copy.65), calls=%async_computation | async-start | bytes 2097152 | tf_op jit(solution)/shard_map/all_to_all | solution.py:121
  61.6 27.1 %all-to-all-start.6 = ((bf16[128,4,1,4,128]{4,1,3,2,0:T(4,128)(2,1)}), bf16[128,4,1,4,128]{4,1,3,2,0:T(4,128)(2,1)S(1)}, u32[]{:S(2)}, u32[]{:S(2)}) async-start(bf16[128,4,1,4,128]{4,1,3,2,0:T(4,128)(2,1)} %copy.71), calls=%async_computation.6 | async-start | bytes 1048576 | tf_op jit(solution)/shard_map/all_to_all | solution.py:110
  88.7 19.3 %all-to-all-start.1 = ((f32[1,4,1,512,128]{4,3,2,0,1:T(8,128)}), f32[1,4,1,512,128]{4,3,2,0,1:T(8,128)S(1)}, u32[]{:S(2)}, u32[]{:S(2)}) async-start(f32[1,4,1,512,128]{4,3,2,0,1:T(8,128)} %copy.66), calls=%async_computation.1 | async-start | bytes 2097152 | tf_op jit(solution)/shard_map/all_to_all | solution.py:120
  108.0 25.0 %all-to-all-start.7 = ((bf16[1,4,1,512,128]{4,3,2,0,1:T(8,128)(2,1)}), bf16[1,4,1,512,128]{4,3,2,0,1:T(8,128)(2,1)S(1)}, u32[]{:S(2)}, u32[]{:S(2)}) async-start(bf16[1,4,1,512,128]{4,3,2,0,1:T(8,128)(2,1)} %copy.72), calls=%async_computation.7 | async-start | bytes 1048576 | tf_op jit(solution)/shard_map/all_to_all | solution.py:109
  111.5 0.7 copy-start.5
  133.8 21.5 %all-to-all-start.4 = ((f32[1,128,4,4,1]{2,3,4,0,1:T(4,128)}), f32[1,128,4,4,1]{2,3,4,0,1:T(4,128)S(1)}, u32[]{:S(2)}, u32[]{:S(2)}) async-start(f32[1,128,4,4,1]{2,3,4,0,1:T(4,128)} %broadcast_in_dim.62), calls=%async_computation.4 | async-start | bytes 524288 | tf_op jit(solution)/shard_map/all_to_all | solution.py:75
  155.3 36.6 %all-to-all-start.2 = ((f32[1,128,4,4,128]{4,3,2,0,1:T(4,128)}), f32[1,128,4,4,128]{4,3,2,0,1:T(4,128)S(1)}, u32[]{:S(2)}, u32[]{:S(2)}) async-start(f32[1,128,4,4,128]{4,3,2,0,1:T(4,128)} %reshape.354), calls=%async_computation.2 | async-start | bytes 2097152 | tf_op jit(solution)/shard_map/all_to_all | solution.py:68
  160.9 68.7 %all-gather.3.cloned.1.call-start = ((), (), s32[]{:S(2)}) async-start(), calls=%async_computation.8 | async-start | bytes 1310720 | tf_op jit(solution)/shard_map/all_gather | solution.py:154
  160.9 15.0 %collective-permute-start = (bf16[512,512]{1,0:T(8,128)(2,1)}, bf16[512,512]{1,0:T(8,128)(2,1)S(1)}, u32[]{:S(2)}, u32[]{:S(2)}) collective-permute-start(bf16[512,512]{1,0:T(8,128)(2,1)} %get-tuple-element.45), channel_id=1, source_target_pairs={{0,1},{1,0},{2,3},{3,2},{4,5},{5,4},{6,7},{7,6},{8,9},{9,8},{10,11... | collective-permute-start | bytes 1572872 | tf_op jit(solution)/shard_map/ppermute | solution.py:17
  191.9 8.7 %all-to-all-start.5 = ((f32[128,1,4,4,1]{0,2,4,1,3:T(4,128)}), f32[128,1,4,4,1]{0,2,4,1,3:T(4,128)S(1)}, u32[]{:S(2)}, u32[]{:S(2)}) async-start(f32[128,1,4,4,1]{0,2,4,1,3:T(4,128)} %copy.68), calls=%async_computation.5 | async-start | bytes 16384 | tf_op jit(solution)/shard_map/all_to_all | solution.py:74
  200.6 29.0 %all-to-all-start.3 = ((f32[128,1,4,4,128]{4,2,0,1,3:T(4,128)}), f32[128,1,4,4,128]{4,2,0,1,3:T(4,128)S(1)}, u32[]{:S(2)}, u32[]{:S(2)}) async-start(f32[128,1,4,4,128]{4,2,0,1,3:T(4,128)} %copy.67), calls=%async_computation.3 | async-start | bytes 2097152 | tf_op jit(solution)/shard_map/all_to_all | solution.py:67
  204.2 0.7 copy-start.4
  229.7 19.9 %copy-start.3 = (bf16[4,256,512]{2,1,0:T(8,128)(2,1)S(1)}, bf16[4,256,512]{2,1,0:T(8,128)(2,1)}, u32[]{:S(2)}) copy-start(bf16[4,256,512]{2,1,0:T(8,128)(2,1)} %all-gather.3.cloned.1.call-done) | copy-start | bytes 3145732
  249.6 1.1 copy-start.1
Sparse Core Ops, SparseCore 0:
  179.0 28.8 all-gather.2
where the time goes:
time: 260 us; the launch traced here: 258 us
  waiting for transfers between devices  102 us (39%)
  local copies, waits for them, and re-layouts  69 us (27%)
  starting transfers between devices  55.8 us (21%)
  between operations  15 us (6%)
  matrix products  13 us (5%)
    all_to_all x1, waiting for transfers between devices, per_device(): lax.all_to_all(packed, 'wide', split_axis=0, concat_axis=3, tiled=True)  27.8 us
    scatter x1, local copies, waits for them, and re-layouts, return_rows(): blank_diag.at[target, side_grid].set(incoming_diag, mode='drop')  23.8 us
    scatter x1, local copies, waits for them, and re-layouts, return_rows(): placed_roots = blank_roots.at[target, side_grid].set(incoming, mode='drop')  19.9 us
    all_to_all x1, waiting for transfers between devices, per_device(): lax.all_to_all(grad_packed, 'wide', split_axis=0, concat_axis=3, tiled=True)  19.5 us
    all_to_all x1, starting transfers between devices, per_device(): lax.all_to_all(packed, 'wide', split_axis=0, concat_axis=3, tiled=True)  18.6 us
    all_to_all x1, waiting for transfers between devices, per_device(): lax.all_to_all(lax.all_to_all(packed, 'wide', split_axis=0, concat_axis=3...  14.4 us
    all_to_all x1, waiting for transfers between devices, return_rows(): lax.all_to_all(diag_out, 'wide', split_axis=1, concat_axis=0, tiled=True)  14 us
    all_to_all x1, waiting for transfers between devices, return_rows(): lax.all_to_all(outgoing, 'wide', split_axis=1, concat_axis=0, tiled=True)  12.3 us
  transfers between devices with their start and end apart: 10, of which 7 were waited for; matrix products, arithmetic and copies ran while one was open for 21% of the time, Pallas kernels for 0%

commit v1 on v0

v1 whole, which is shorter than its diff:
```python
import jax
import jax.numpy as jnp
from jax import lax
from jax.experimental import pallas as pl
from jax.experimental.pallas import tpu as pltpu
from jax.sharding import PartitionSpec as P

BLOCK = 512
CHIPS = 64
NARROW = 4
MESH = pl.DeviceIdType.MESH
F32 = jnp.float32
BF16 = jnp.bfloat16


def dot(first, second):
    return jnp.dot(first, second, preferred_element_type=F32)


def dot_nt(first, second):
    return lax.dot_general(
        first, second, (((1,), (1,)), ((), ())), preferred_element_type=F32
    )


def iota(shape, axis):
    return lax.broadcasted_iota(jnp.int32, shape, axis)


def send(src, dst, send_sem, recv_sem, wide, narrow):
    pltpu.make_async_remote_copy(
        src_ref=src,
        dst_ref=dst,
        send_sem=send_sem,
        recv_sem=recv_sem,
        device_id=(wide, narrow),
        device_id_type=MESH,
    ).start()


def wait(ref, sem):
    pltpu.make_async_copy(ref, ref, sem).wait()


def kernel(
    stat_ref,
    grad_ref,
    assign_ref,
    counts_ref,
    counts_smem,
    roots_ref,
    diag_ref,
    dirs_ref,
    out1,
    in1,
    flat1,
    out2,
    in2,
    gflat,
    gout1,
    gin1,
    gflat1,
    gout2,
    gin2,
    grad_half,
    factor,
    work,
    low_a,
    low_b,
    low_root,
    half_out,
    half_in,
    dir_out,
    out3,
    in3,
    flat3,
    out4,
    in4,
    select_t,
    send1,
    recv1,
    send2,
    recv2,
    gsend1,
    grecv1,
    gsend2,
    grecv2,
    half_send,
    half_recv,
    prod_send,
    prod_recv,
    dir_send,
    dir_recv,
    send3,
    recv3,
    send4,
    recv4,
):
    wide = lax.axis_index("wide")
    me_n = lax.axis_index("narrow")
    me_j = wide // 2
    me_c = wide % 2
    me_y = me_j % 8
    me_z = me_j // 8
    me_g = me_n * 2 + me_c

    def group_mate(i):
        g = lax.rem(me_g + i, 8)
        return g, me_j * 2 + g % 2, g // 2

    def far_mate(i):
        y = lax.rem(me_y + i % 8, 8)
        z = lax.rem(me_z + i // 8, 8)
        return z * 8 + y

    barrier = pltpu.get_barrier_semaphore()

    @pl.loop(1, 64)
    def _(i):
        pl.semaphore_signal(
            barrier, inc=1, device_id=(far_mate(i) * 2 + me_c, me_n), device_id_type=MESH
        )

    @pl.loop(1, 8)
    def _(i):
        _, w, n = group_mate(i)
        pl.semaphore_signal(barrier, inc=1, device_id=(w, n), device_id_type=MESH)

    block_of_row = iota((128, 128), 0)
    one_hots = []
    picks = []
    for slot in range(2):
        listed = assign_ref[slot : slot + 1, :]
        hot = block_of_row == listed
        one_hots.append(jnp.where(hot, 1.0, 0.0).astype(BF16))
        kept = jnp.logical_and(hot, counts_ref[...] > slot)
        picks.append(jnp.where(kept, 1.0, 0.0).astype(BF16))
    gathers = []
    for m in range(4):
        par, slot = m // 2, m % 2
        spread = jnp.where(
            iota((CHIPS, 128), 1) == 2 * iota((CHIPS, 128), 0) + par, 1.0, 0.0
        ).astype(BF16)
        gathers.append(dot_nt(spread, one_hots[slot]).astype(BF16))
        spread_t = jnp.where(
            iota((128, 128), 0) == 2 * iota((128, 128), 1) + par, 1.0, 0.0
        ).astype(BF16)
        select_t[:, 128 * m : 128 * m + 128] = dot(picks[slot], spread_t).astype(BF16)
    gather = jnp.concatenate(gathers, axis=0)

    for k in range(2):
        for r in range(4):
            x = stat_ref[pl.ds(k * 4 + r, 128, stride=8), :]
            high = x.astype(BF16)
            rest = (x - high.astype(F32)).astype(BF16)
            upper = iota((128, 128), 1) + 128 * me_n >= 4 * wide + r
            mixed = jnp.where(upper, high.astype(F32), rest.astype(F32)).astype(BF16)
            picked = dot(gather, mixed).astype(BF16)
            for m in range(4):
                out1[m * 2 + k, r * 64 : r * 64 + 64, :] = picked[m * 64 : m * 64 + 64]
    gflat[...] = grad_ref[...].astype(F32)
    for r in range(4):
        x = gflat[pl.ds(r, 128, stride=4), :].astype(BF16)
        picked = dot(gather, x).astype(BF16)
        for m in range(4):
            gout1[m, r * 64 : r * 64 + 64, :] = picked[m * 64 : m * 64 + 64]
    in1[me_g] = out1[me_g]

    pl.semaphore_wait(barrier, 70)

    @pl.loop(1, 8)
    def _(i):
        g, w, n = group_mate(i)
        send(out1.at[g], in1.at[me_g], send1, recv1, w, n)

    g_core = me_n // 2
    g_place = (me_n % 2) * 2 + me_c
    for d in range(1, 4):
        m = lax.rem(me_n + d, 4)
        send(gout1.at[m], gin1.at[g_place], gsend1, grecv1, me_j * 2 + g_core, m)

    @pl.when(g_core != me_c)
    def _():
        send(gout1.at[me_n], gin1.at[g_place], gsend1, grecv1, me_j * 2 + g_core, me_n)

    @pl.when(g_core == me_c)
    def _():
        gin1[g_place] = gout1[me_n]

    wait(in1.at[pl.ds(0, 7)], recv1)
    for g in range(8):
        flat1[g * 256 : g * 256 + 256, :] = in1[g].astype(F32)

    @pl.loop(0, CHIPS, unroll=8)
    def _(i):
        out2[i] = flat1[pl.ds(i, 32, stride=64), :].astype(BF16)

    in2[me_j] = out2[me_j]

    @pl.loop(1, CHIPS)
    def _(i):
        j = far_mate(i)
        send(out2.at[j], in2.at[me_j], send2, recv2, j * 2 + me_c, me_n)

    @pl.when(g_core == me_c)
    def _():
        wait(gin1.at[pl.ds(0, 3)], grecv1)

    @pl.when(g_core != me_c)
    def _():
        wait(gin1, grecv1)

    for g in range(4):
        gflat1[g * 256 : g * 256 + 256, :] = gin1[g].astype(F32)

    @pl.loop(0, CHIPS, unroll=8)
    def _(i):
        gout2[i] = gflat1[pl.ds(i, 16, stride=64), :].astype(BF16)

    gin2[me_j] = gout2[me_j]

    @pl.loop(1, CHIPS)
    def _(i):
        j = far_mate(i)
        send(gout2.at[j], gin2.at[me_j], gsend2, grecv2, j * 2 + me_c, me_n)

    wait(in2.at[pl.ds(0, CHIPS - 1)], recv2)

    @pl.loop(0, CHIPS, unroll=4)
    def _(i):
        x = in2[i].astype(F32)
        rows = pl.ds(pl.multiple_of(i * 8, 8), 8)
        for n in range(4):
            factor[rows, 128 * n : 128 * n + 128] = x[8 * n : 8 * n + 8]

    eye = iota((BLOCK, BLOCK), 0) == iota((BLOCK, BLOCK), 1)
    received = factor[...]
    a = received + jnp.where(eye, 0.0, received.T)
    total = jnp.sum(jnp.sum(a * a, axis=0, keepdims=True), axis=1, keepdims=True)
    scaling = 2.5 / jnp.sqrt(total)
    c = scaling * a
    factor[...] = c
    low_a[...] = c.astype(BF16)
    e = dot(low_a[...], low_a[...]) - 10.0 * factor[...]
    work[...] = e
    low_b[...] = e.astype(BF16)
    f = 50.0 * work[...] + dot(low_b[...], low_b[...])
    low_b[...] = f.astype(BF16)
    c2 = (625.0 / 256.0) * factor[...] + (1.0 / 256.0) * dot(low_b[...], low_a[...])
    work[...] = c2
    low_b[...] = c2.astype(BF16)
    scale4 = jnp.sqrt(jnp.sqrt(scaling)) * (1.0 / 16.0)
    tail = dot(low_a[...], low_b[...]) - 5.0 * (factor[...] + work[...])
    root = scale4 * (jnp.where(eye, 25.0, 0.0) + tail)
    work[...] = root
    low_root[...] = root.astype(BF16)

    @pl.loop(0, CHIPS, unroll=4)
    def _(i):
        rows = pl.ds(pl.multiple_of(i * 8, 8), 8)
        parts = [work[rows, 128 * n : 128 * n + 128] for n in range(4)]
        out3[i] = jnp.concatenate(parts, axis=0).astype(BF16)

    in3[me_j] = out3[me_j]

    @pl.loop(1, CHIPS)
    def _(i):
        j = far_mate(i)
        send(out3.at[j], in3.at[me_j], send3, recv3, j * 2 + me_c, me_n)

    wait(gin2.at[pl.ds(0, CHIPS - 1)], grecv2)

    @pl.loop(0, CHIPS // 2, unroll=4)
    def _(i):
        x0 = gin2[2 * i].astype(F32)
        x1 = gin2[2 * i + 1].astype(F32)
        rows = pl.ds(pl.multiple_of(i * 16, 16), 16)
        for n in range(2):
            both = jnp.concatenate([x0[8 * n : 8 * n + 8], x1[8 * n : 8 * n + 8]], axis=0)
            grad_half[me_c, rows, 128 * n : 128 * n + 128] = both.astype(BF16)

    @pl.when(me_c == 1)
    def _():
        send(grad_half.at[1], grad_half.at[1], half_send, half_recv, me_j * 2, me_n)
        wait(half_in, prod_recv)
        product = dot(half_in[...], low_root[...])
        taken = counts_smem[2 * me_j + me_n // 2] > me_n % 2
        product = product * jnp.where(taken, 1.0, 0.0)
        dir_out[...] = product.astype(BF16)
        for d in range(1, 4):
            n = lax.rem(me_n + d, 4)
            send(
                dir_out,
                dirs_ref.at[me_n % 2],
                dir_send,
                dir_recv.at[me_n % 2],
                me_j * 2 + me_n // 2,
                n,
            )

    @pl.when(me_c == 0)
    def _():
        wait(grad_half.at[1], half_recv)
        for k in range(2):
            half_out[:, 256 * k : 256 * k + 256] = dot(low_root[...], grad_half[k]).astype(BF16)
        send(half_out, half_in, prod_send, prod_recv, me_j * 2 + 1, me_n)

    @pl.when(jnp.logical_and(me_c == 1, me_n // 2 == 0))
    def _():
        send(
            dir_out,
            dirs_ref.at[me_n % 2],
            dir_send,
            dir_recv.at[me_n % 2],
            me_j * 2,
            me_n,
        )

    @pl.when(jnp.logical_and(me_c == 1, me_n // 2 == 1))
    def _():
        dirs_ref[me_n % 2] = dir_out[...]

    wait(in3.at[pl.ds(0, CHIPS - 1)], recv3)

    @pl.loop(0, CHIPS, unroll=8)
    def _(i):
        flat3[pl.ds(pl.multiple_of(i * 32, 32), 32), :] = in3[i].astype(F32)

    for q in range(32):
        n, c_, r = q // 8, (q // 4) % 2, q % 4
        out4[n * 2 + c_, r * 64 : r * 64 + 64, :] = flat3[pl.ds(q, 64, stride=32), :].astype(BF16)
    for c_ in range(2):
        diag = jnp.zeros((16, 64), F32)
        for r in range(4):
            rows = flat3[pl.ds((me_j // 16) * 8 + c_ * 4 + r, 64, stride=32), :].astype(BF16)
            place = jnp.logical_and(
                iota((16, 128), 0) == r, iota((16, 128), 1) == (8 * me_j + 4 * c_ + r) % 128
            )
            diag = diag + dot_nt(jnp.where(place, 1.0, 0.0).astype(BF16), rows)
        padded = jnp.concatenate([diag, jnp.zeros((16, 64), F32)], axis=1).astype(BF16)
        for n in range(4):
            out4[n * 2 + c_, 256:272, :] = padded
    in4[me_g] = out4[me_g]

    @pl.loop(1, 8)
    def _(i):
        g, w, n = group_mate(i)
        send(out4.at[g], in4.at[me_g], send4, recv4, w, n)

    wait(in4.at[pl.ds(0, 7)], recv4)
    for k in range(2):
        for r in range(4):
            acc = jnp.zeros((128, 128), F32)
            for m in range(4):
                acc = acc + dot(
                    select_t[:, 128 * m : 128 * m + 64], in4[m * 2 + k, r * 64 : r * 64 + 64, :]
                )
            on_diag = iota((128, 128), 1) + 128 * me_n == 4 * wide + r
            roots_ref[pl.ds(k * 4 + r, 128, stride=8), :] = jnp.where(on_diag, 0.0, acc)
        dg = jnp.zeros((128, 16), F32)
        for m in range(4):
            dg = dg + dot_nt(select_t[:, 128 * m : 128 * m + 128], in4[m * 2 + k, 256:272, :])
        diag_ref[k] = dg

    @pl.when(jnp.logical_and(me_c == 1, me_n == 2))
    def _():
        wait(dirs_ref.at[1], dir_recv.at[1])

    @pl.when(jnp.logical_and(me_c == 1, me_n == 3))
    def _():
        wait(dirs_ref.at[0], dir_recv.at[0])

    @pl.when(jnp.logical_or(me_c == 0, me_n < 2))
    def _():
        wait(dirs_ref.at[0], dir_recv.at[0])
        wait(dirs_ref.at[1], dir_recv.at[1])

    wait(in1.at[pl.ds(0, 7)], send1)
    wait(in2.at[pl.ds(0, CHIPS - 1)], send2)
    wait(gin2.at[pl.ds(0, CHIPS - 1)], gsend2)
    wait(in3.at[pl.ds(0, CHIPS - 1)], send3)
    wait(in4.at[pl.ds(0, 7)], send4)

    @pl.when(g_core == me_c)
    def _():
        wait(gin1.at[pl.ds(0, 3)], gsend1)

    @pl.when(g_core != me_c)
    def _():
        wait(gin1, gsend1)

    @pl.when(me_c == 0)
    def _():
        wait(half_in, prod_send)

    @pl.when(me_c == 1)
    def _():
        wait(grad_half.at[1], half_send)

    @pl.when(jnp.logical_and(me_c == 1, me_n // 2 == 0))
    def _():
        wait(dirs_ref, dir_send)
        wait(dirs_ref, dir_send)

    @pl.when(jnp.logical_and(me_c == 1, me_n // 2 == 1))
    def _():
        wait(dirs_ref, dir_send)
        wait(dirs_ref.at[0], dir_send)


def per_device(statistics, gradients, assign, counts):
    blocks = statistics.shape[0]
    vmem = pl.BlockSpec(memory_space=pltpu.VMEM)
    smem = pl.BlockSpec(memory_space=pltpu.SMEM)
    square = (BLOCK, BLOCK)
    scratch = [
        pltpu.VMEM((8, 256, 128), BF16),
        pltpu.VMEM((8, 256, 128), BF16),
        pltpu.VMEM((2048, 128), F32),
        pltpu.VMEM((64, 32, 128), BF16),
        pltpu.VMEM((64, 32, 128), BF16),
        pltpu.VMEM((512, 128), F32),
        pltpu.VMEM((4, 256, 128), BF16),
        pltpu.VMEM((4, 256, 128), BF16),
        pltpu.VMEM((1024, 128), F32),
        pltpu.VMEM((64, 16, 128), BF16),
        pltpu.VMEM((64, 16, 128), BF16),
        pltpu.VMEM((2, BLOCK, 256), BF16),
        pltpu.VMEM(square, F32),
        pltpu.VMEM(square, F32),
        pltpu.VMEM(square, BF16),
        pltpu.VMEM(square, BF16),
        pltpu.VMEM(square, BF16),
        pltpu.VMEM(square, BF16),
        pltpu.VMEM(square, BF16),
        pltpu.VMEM(square, BF16),
        pltpu.VMEM((64, 32, 128), BF16),
        pltpu.VMEM((64, 32, 128), BF16),
        pltpu.VMEM((2048, 128), F32),
        pltpu.VMEM((8, 272, 128), BF16),
        pltpu.VMEM((8, 272, 128), BF16),
        pltpu.VMEM((128, 512), BF16),
    ]
    dma = pltpu.SemaphoreType.DMA
    scratch += [dma] * 12 + [dma, dma((2,))] + [dma] * 4
    roots, diags, dirs = pl.pallas_call(
        kernel,
        out_shape=[
            jax.ShapeDtypeStruct((blocks * 8, 128), F32),
            jax.ShapeDtypeStruct((2, blocks, 16), F32),
            jax.ShapeDtypeStruct((2, BLOCK, BLOCK), BF16),
        ],
        in_specs=[vmem, vmem, vmem, vmem, smem],
        out_specs=[vmem, vmem, vmem],
        scratch_shapes=scratch,
        compiler_params=pltpu.CompilerParams(
            collective_id=0, has_side_effects=True, vmem_limit_bytes=48 * 2**20
        ),
        cost_estimate=pl.CostEstimate(
            flops=2 * 6 * BLOCK**3, bytes_accessed=4 * 2**20, transcendentals=0
        ),
        name="shampoo_roots",
    )(
        statistics.reshape(blocks * 8, 128),
        gradients.reshape(blocks * 4, 128),
        assign.T,
        counts.reshape(1, -1),
        counts,
    )
    inverse_roots = roots.reshape(statistics.shape)
    root_diagonals = jnp.swapaxes(diags[:, :, :4], 0, 1)
    return inverse_roots, root_diagonals, dirs[None]


def solution(mesh):
    return jax.shard_map(
        per_device,
        mesh=mesh,
        in_specs=(P(None, None, "wide", "narrow"), P(None, "wide", "narrow"), P(), P()),
        out_specs=(
            P(None, None, "wide", "narrow"),
            P(None, None, "wide"),
            P("wide", None, None, None),
        ),
        check_vma=False,
    )
```

time: 260 us -> 91.8 us (0.35)
  waiting for transfers between devices: 102 us -> 0 us
  Pallas kernels: 0 us -> 85.5 us
  local copies, waits for them, and re-layouts: 69 us -> 5.06 us
  starting transfers between devices: 55.8 us -> 0 us
  between operations: 15 us -> 0.67 us
  matrix products: 13 us -> 0 us
    all_to_all x8 -> x0, waiting for transfers between devices: 91 us -> none  [the longest x1 27.8 us: per_device(): lax.all_to_all(packed, 'wide', split_axis=0, concat_axis=3, tiled=True)]
    pallas_call x0 -> x1, Pallas kernels: none -> 85.5 us  [per_device(): pl.pallas_call(kernel, out_shape=[jax.ShapeDtypeStruct((blocks * 8, 128),...]
    all_to_all x8 -> x0, starting transfers between devices: 52.2 us -> none  [the longest x1 18.6 us: per_device(): lax.all_to_all(packed, 'wide', split_axis=0, concat_axis=3, tiled=True)]
    scatter x2 -> x0, local copies, waits for them, and re-layouts: 43.6 us -> none  [the longest x1 23.8 us: return_rows(): blank_diag.at[target, side_grid].set(incoming_diag, mode='drop')]
    dot_general x5 -> x0, matrix products: 13 us -> none  [the longest x4 11.2 us: batched_product(): jnp.einsum('kij,kjl->kil', first, second, precision=lax.Precision.HIGHEST...]
    ppermute x1 -> x0, waiting for transfers between devices: 11.4 us -> none  [partner_2(): return lax.ppermute(block, axis, route)]
    gather x3 -> x0, local copies, waits for them, and re-layouts: 9.08 us -> none  [the longest x1 4.51 us: return_rows(): diagonal = jnp.diagonal(own_root).reshape(wide_count, shard_rows)]
    all_to_all x5 -> x0, local copies, waits for them, and re-layouts: 4.2 us -> none  [the longest x1 1.24 us: return_rows(): lax.all_to_all(outgoing, 'wide', split_axis=1, concat_axis=0, tiled=True)]
  transfers between devices with their start and end apart: 10 -> 0, of which waited for: 7 -> 0; matrix products, arithmetic and copies ran while one was open for 21% -> 0% of each run, Pallas kernels for 0% -> 0%
where the time goes in v1:
time: 91.8 us; the launch traced here: 91.3 us
  Pallas kernels  85.5 us (93%)
  local copies, waits for them, and re-layouts  5.06 us (6%)
    pallas_call x1, Pallas kernels, per_device(): pl.pallas_call(kernel, out_shape=[jax.ShapeDtypeStruct((blocks * 8, 128),...  85.5 us
    unnamed x11, local copies, waits for them, and re-layouts  5.05 us

profile of v1, /device:TPU:1, one launch (start us, length us, event | category | flops | bytes accessed | tf_op | source)
XLA Modules:
  0.0 91.3 jit_solution(18267293113827036640)
XLA Ops:
  0.6 0.0 copy-start.2
  0.6 0.0 copy-start.3
  0.7 0.7 copy-done.2
  1.3 0.0 copy-done.3
  1.3 0.0 copy-start
  1.3 1.0 %copy-done = f32[128,2,4,128]{3,2,1,0:T(4,128)S(1)} copy-done((f32[128,2,4,128]{3,2,1,0:T(4,128)S(1)}, f32[128,2,4,128]{3,2,1,0:T(4,128)}, u32[]{:S(2)}) %copy-start) | copy-done | bytes 524312
  2.4 0.0 copy-start.1
  2.4 0.9 copy-done.1
  3.3 85.5 %shampoo_roots.1 = (f32[1024,128]{1,0:T(8,128)S(1)}, f32[2,128,16]{2,1,0:T(8,128)S(1)}, bf16[2,512,512]{2,1,0:T(8,128)(2,1)S(1)}) custom-call(f32[1024,128]{1,0:T(8,128)S(1)} %bitcast.10, bf16[512,128]{1,0:T(8,128)(2,1)S(1)} %bitcast.11, s32[2,128]{1,0:T(2,128)S(1)} %bitcast.12, s32[1,128]{1,0:T(1,128)S(1)} %bitcast.13, s32[128]{0:T(128)S(1)} %copy-done.3), custom_call_target="tpu_custom_call" | custom-call | flops 1610612736 | bytes 4194304 | tf_op jit(solution)/shard_map/shampoo_roots/pallas_call | solution.py:446
  88.8 0.7 copy.7
  89.5 0.8 copy.10
  90.3 1.0 %copy.11 = bf16[1,2,512,512]{3,2,1,0:T(8,128)(2,1)} copy(bf16[1,2,512,512]{3,2,1,0:T(8,128)(2,1)S(1)} %bitcast.8) | data formatting | bytes 2097152
  (1 shorter events, 0.0 us)
Async XLA Ops:
  0.6 0.7 copy-start.2
  0.6 0.7 copy-start.3
  1.3 1.0 %copy-start = (f32[128,2,4,128]{3,2,1,0:T(4,128)S(1)}, f32[128,2,4,128]{3,2,1,0:T(4,128)}, u32[]{:S(2)}) copy-start(f32[128,2,4,128]{3,2,1,0:T(4,128)} %param.4) | copy-start | bytes 1572868
  2.4 0.9 copy-start.1

commit v2 on v1

v2 whole, which is shorter than its diff:
```python
import jax
import jax.numpy as jnp
from jax import lax
from jax.experimental import pallas as pl
from jax.experimental.pallas import tpu as pltpu
from jax.sharding import PartitionSpec as P

BLOCK = 512
CHIPS = 64
MESH = pl.DeviceIdType.MESH
F32 = jnp.float32
BF16 = jnp.bfloat16

OWN = 48


def steps(place):
    return place % 8, (place // 8 + 2) % 8


def distance(place):
    return sum(min(s, 8 - s) for s in steps(place))


FAR = sorted(range(32), key=lambda p: -distance(p))
NEAR = sorted((p for p in range(32, 64) if p != OWN), key=lambda p: -distance(p))


def dot(first, second):
    return jnp.dot(first, second, preferred_element_type=F32)


def dot_nt(first, second):
    return lax.dot_general(
        first, second, (((1,), (1,)), ((), ())), preferred_element_type=F32
    )


def iota(shape, axis):
    return lax.broadcasted_iota(jnp.int32, shape, axis)


def hot(condition):
    return jnp.where(condition, 1.0, 0.0).astype(BF16)


def send(src, dst, send_sem, recv_sem, wide, narrow):
    pltpu.make_async_remote_copy(
        src_ref=src,
        dst_ref=dst,
        send_sem=send_sem,
        recv_sem=recv_sem,
        device_id=(wide, narrow),
        device_id_type=MESH,
    ).start()


def wait(ref, sem):
    pltpu.make_async_copy(ref, ref, sem).wait()


def kernel(
    stat_hbm,
    grad_hbm,
    assign_hbm,
    counts_hbm,
    roots_ref,
    diag_ref,
    dirs_ref,
    stat_ref,
    grad_ref,
    assign_ref,
    counts_ref,
    out1,
    in1,
    flat1,
    out2,
    in2,
    gflat,
    gspread,
    gout1,
    gin1,
    gmid,
    gout2,
    gin2,
    grows,
    grad,
    factor,
    work,
    low_a,
    low_b,
    low_root,
    half_out,
    half_in,
    dir_out,
    out3,
    in3,
    flat3,
    out4a,
    in4a,
    out4b,
    in4b,
    partial,
    load_sem,
    send1,
    recv1,
    send2,
    recv2,
    gsend1,
    grecv1,
    gsend2,
    grecv2,
    prod_send,
    prod_recv,
    dir_send,
    dir_recv,
    send3,
    recv3,
    send4,
    recv4,
):
    loads = [
        pltpu.make_async_copy(src, dst, load_sem.at[i])
        for i, (src, dst) in enumerate(
            [
                (assign_hbm, assign_ref),
                (counts_hbm, counts_ref),
                (stat_hbm, stat_ref),
                (grad_hbm, grad_ref),
            ]
        )
    ]
    for load in loads:
        load.start()
    wide = lax.axis_index("wide")
    me_n = lax.axis_index("narrow")
    me_j = wide // 2
    me_c = wide % 2
    me_y = me_j % 8
    me_z = me_j // 8
    me_g = me_n * 2 + me_c
    along_y = [(me_y + s) % 8 for s in range(8)]
    along_z = [(me_z + s) % 8 * 8 for s in range(8)]

    def chip(place):
        y, z = steps(place)
        return along_z[z] + along_y[y]

    def group_mate(i):
        g = (me_g + i) % 8
        return g, me_j * 2 + g % 2, g // 2

    barrier = pltpu.get_barrier_semaphore()
    for i in range(1, 8):
        _, w, n = group_mate(i)
        pl.semaphore_signal(barrier, inc=1, device_id=(w, n), device_id_type=MESH)
    for place in FAR + NEAR:
        pl.semaphore_signal(
            barrier, inc=1, device_id=(chip(place) * 2 + me_c, me_n), device_id_type=MESH
        )

    def chips_at(shape, axis, sign):
        place = iota(shape, axis)
        y, z = place % 8, (place // 8 + 2) % 8
        return (me_z + sign * z + 8) % 8 * 8 + (me_y + sign * y + 8) % 8

    loads[0].wait()
    loads[1].wait()
    to_worker = 2 * chips_at((CHIPS, 128), 0, 1)
    from_worker = 2 * chips_at((128, CHIPS), 1, -1)
    listed = []
    taken = []
    for slot in range(2):
        match = iota((128, 128), 0) == assign_ref[slot : slot + 1, :]
        listed.append(hot(match))
        taken.append(hot(jnp.logical_and(match, counts_ref[...] > slot)))
    gathers = []
    selects = []
    for m in range(4):
        par, slot = m // 2, m % 2
        pick = hot(iota((CHIPS, 128), 1) == to_worker + par)
        gathers.append(dot_nt(pick, listed[slot]).astype(BF16))
        place = hot(iota((128, CHIPS), 0) == from_worker + par)
        selects.append(dot(taken[slot], place).astype(BF16))
    gather = jnp.concatenate(gathers, axis=0)

    loads[2].wait()
    for k in range(2):
        for r in range(4):
            x = stat_ref[pl.ds(k * 4 + r, 128, stride=8), :]
            high = x.astype(BF16).astype(F32)
            upper = iota((128, 128), 1) + 128 * me_n >= 4 * wide + r
            mixed = jnp.where(upper, high, x - high).astype(BF16)
            picked = dot(gather, mixed).astype(BF16)
            for m in range(4):
                for half in range(2):
                    start = m * 64 + half * 32
                    out1[half, m * 2 + k, r * 32 : r * 32 + 32, :] = picked[start : start + 32]
    for half in range(2):
        in1[half, me_g] = out1[half, me_g]
    loads[3].wait()
    gflat[...] = grad_ref[...].astype(F32)
    for r in range(4):
        x = gflat[pl.ds(r, 128, stride=4), :].astype(BF16)
        picked = dot(gather, x)
        for m in range(4):
            gspread[pl.ds(m * 4 + r, 64, stride=16), :] = picked[m * 64 : m * 64 + 64]
    gout1[...] = gspread[...].reshape(CHIPS, 16, 128).astype(BF16)
    gin1[me_j] = gout1[OWN]

    pl.semaphore_wait(barrier, 70)

    for half in range(2):
        for i in (4, 5, 3, 2, 6, 7, 1):
            g, w, n = group_mate(i)
            send(
                out1.at[half, g], in1.at[half, me_g], send1.at[half], recv1.at[half], w, n
            )
    for place in FAR + NEAR:
        send(
            gout1.at[place], gin1.at[me_j], gsend1, grecv1, chip(place) * 2 + me_c, me_n
        )

    for half, places in enumerate((FAR, NEAR)):
        wait(in1.at[half, pl.ds(0, 7)], recv1.at[half])
        flat1[half] = in1[half].reshape(1024, 128).astype(F32)
        if half == 1:
            out2[OWN] = flat1[1, pl.ds(OWN - 32, 32, stride=32), :].astype(BF16)
            in2[me_j] = out2[OWN]
        for place in places:
            out2[place] = flat1[half, pl.ds(place % 32, 32, stride=32), :].astype(BF16)
            send(
                out2.at[place], in2.at[me_j], send2, recv2, chip(place) * 2 + me_c, me_n
            )

    wait(gin1.at[pl.ds(0, CHIPS - 1)], grecv1)
    gmid[...] = gin1[...].reshape(1024, 128).astype(F32)
    for m in range(4):
        for r in range(4):
            gout2[m, r * 64 : r * 64 + 64, :] = gmid[pl.ds(m * 4 + r, 64, stride=16), :].astype(
                BF16
            )
    for d in (2, 1, 3):
        m = (me_n + d) % 4
        send(gout2.at[m], gin2.at[me_g], gsend2, grecv2, me_j * 2, m)

    @pl.when(me_c == 1)
    def _():
        send(gout2.at[me_n], gin2.at[me_g], gsend2, grecv2, me_j * 2, me_n)

    @pl.when(me_c == 0)
    def _():
        gin2[me_g] = gout2[me_n]

    wait(in2.at[pl.ds(0, CHIPS - 1)], recv2)
    for j in range(CHIPS):
        x = in2[j].astype(F32)
        for n in range(4):
            factor[8 * j : 8 * j + 8, 128 * n : 128 * n + 128] = x[8 * n : 8 * n + 8]

    eye = iota((BLOCK, BLOCK), 0) == iota((BLOCK, BLOCK), 1)
    received = factor[...]
    a = received + jnp.where(eye, 0.0, received.T)
    total = jnp.sum(jnp.sum(a * a, axis=0, keepdims=True), axis=1, keepdims=True)
    scaling = 2.5 / jnp.sqrt(total)
    c = scaling * a
    factor[...] = c
    low_a[...] = c.astype(BF16)
    e = dot(low_a[...], low_a[...]) - 10.0 * factor[...]
    work[...] = e
    low_b[...] = e.astype(BF16)
    f = 50.0 * work[...] + dot(low_b[...], low_b[...])
    low_b[...] = f.astype(BF16)
    c2 = (625.0 / 256.0) * factor[...] + (1.0 / 256.0) * dot(low_b[...], low_a[...])
    work[...] = c2
    low_b[...] = c2.astype(BF16)
    scale4 = jnp.sqrt(jnp.sqrt(scaling)) * (1.0 / 16.0)
    tail = dot(low_a[...], low_b[...]) - 5.0 * (factor[...] + work[...])
    root = scale4 * (jnp.where(eye, 25.0, 0.0) + tail)
    work[...] = root
    low_root[...] = root.astype(BF16)

    def rows_for(place):
        rows = pl.ds(pl.multiple_of(chip(place) * 8, 8), 8)
        parts = [work[rows, 128 * n : 128 * n + 128] for n in range(4)]
        return jnp.concatenate(parts, axis=0).astype(BF16)

    for half, places in enumerate((FAR, NEAR)):
        for place in places:
            out3[place] = rows_for(place)
            send(
                out3.at[place],
                in3.at[place],
                send3.at[half],
                recv3.at[half],
                chip(place) * 2 + me_c,
                me_n,
            )
    in3[OWN] = rows_for(OWN)

    @pl.when(me_c == 0)
    def _():
        wait(gin2.at[pl.ds(0, 7)], grecv2)
        for g in range(8):
            for r in range(4):
                grows[g // 2, pl.ds(g % 2 * 4 + r, 64, stride=8), :] = gin2[
                    g, r * 64 : r * 64 + 64, :
                ].astype(F32)
        for n in range(4):
            grad[:, 128 * n : 128 * n + 128] = grows[n].astype(BF16)
        half_out[...] = dot(low_root[...], grad[...]).astype(BF16)
        send(half_out, half_in, prod_send, prod_recv, me_j * 2 + 1, me_n)

    @pl.when(me_c == 1)
    def _():
        mine = jnp.logical_and(
            iota((1, 128), 1) == 2 * me_j + me_n // 2, counts_ref[...] > me_n % 2
        )
        keep = jnp.sum(jnp.where(mine, 1.0, 0.0), axis=1, keepdims=True)
        wait(half_in, prod_recv)
        dir_out[...] = (dot(half_in[...], low_root[...]) * keep).astype(BF16)
        for d in (2, 1, 3):
            send(
                dir_out,
                dirs_ref.at[me_n % 2],
                dir_send,
                dir_recv.at[me_n % 2],
                me_j * 2 + me_n // 2,
                (me_n + d) % 4,
            )

    @pl.when(jnp.logical_and(me_c == 1, me_n // 2 == 0))
    def _():
        send(
            dir_out,
            dirs_ref.at[me_n % 2],
            dir_send,
            dir_recv.at[me_n % 2],
            me_j * 2,
            me_n,
        )

    @pl.when(jnp.logical_and(me_c == 1, me_n // 2 == 1))
    def _():
        dirs_ref[me_n % 2] = dir_out[...]

    wait(in3.at[pl.ds(0, 32)], recv3.at[0])
    flat3[:1024] = in3[:32].reshape(1024, 128).astype(F32)
    for q in range(32):
        out4a[q // 4, q % 4 * 32 : q % 4 * 32 + 32, :] = flat3[pl.ds(q, 32, stride=32), :].astype(
            BF16
        )
    in4a[me_g] = out4a[me_g]
    for i in (4, 5, 3, 2, 6, 7, 1):
        g, w, n = group_mate(i)
        send(out4a.at[g], in4a.at[me_g], send4.at[0], recv4.at[0], w, n)

    wait(in3.at[pl.ds(0, 31)], recv3.at[1])
    flat3[1024:] = in3[32:].reshape(1024, 128).astype(F32)
    for q in range(32):
        out4b[q // 4, q % 4 * 32 : q % 4 * 32 + 32, :] = flat3[
            pl.ds(1024 + q, 32, stride=32), :
        ].astype(BF16)
    for core in range(2):
        diag = jnp.zeros((16, CHIPS), F32)
        for r in range(4):
            rows = flat3[pl.ds((me_j // 16) * 8 + core * 4 + r, CHIPS, stride=32), :].astype(BF16)
            place = jnp.logical_and(
                iota((16, 128), 0) == r, iota((16, 128), 1) == (8 * me_j + 4 * core + r) % 128
            )
            diag = diag + dot_nt(hot(place), rows)
        padded = jnp.concatenate([diag, jnp.zeros((16, CHIPS), F32)], axis=1).astype(BF16)
        for n in range(4):
            out4b[n * 2 + core, 128:144, :] = padded
    in4b[me_g] = out4b[me_g]
    for i in (4, 5, 3, 2, 6, 7, 1):
        g, w, n = group_mate(i)
        send(out4b.at[g], in4b.at[me_g], send4.at[1], recv4.at[1], w, n)

    def picked_rows(received, k, r, half):
        select = jnp.concatenate([s[:, half * 32 : half * 32 + 32] for s in selects], axis=1)
        rows = [received[m * 2 + k, r * 32 : r * 32 + 32, :] for m in range(4)]
        return dot(select, jnp.concatenate(rows, axis=0))

    wait(in4a.at[pl.ds(0, 7)], recv4.at[0])
    for k in range(2):
        for r in range(4):
            partial[k * 4 + r] = picked_rows(in4a, k, r, 0)
    wait(in4b.at[pl.ds(0, 7)], recv4.at[1])
    for k in range(2):
        for r in range(4):
            full = partial[k * 4 + r] + picked_rows(in4b, k, r, 1)
            on_diag = iota((128, 128), 1) + 128 * me_n == 4 * wide + r
            roots_ref[pl.ds(k * 4 + r, 128, stride=8), :] = jnp.where(on_diag, 0.0, full)
        diag = jnp.zeros((16, 128), F32)
        for m in range(4):
            diag = diag + dot_nt(in4b[m * 2 + k, 128:144, :][:, :CHIPS], selects[m])
        diag_ref[k] = diag[:4]

    @pl.when(jnp.logical_and(me_c == 1, me_n == 2))
    def _():
        wait(dirs_ref.at[1], dir_recv.at[1])

    @pl.when(jnp.logical_and(me_c == 1, me_n == 3))
    def _():
        wait(dirs_ref.at[0], dir_recv.at[0])

    @pl.when(jnp.logical_or(me_c == 0, me_n < 2))
    def _():
        wait(dirs_ref.at[0], dir_recv.at[0])
        wait(dirs_ref.at[1], dir_recv.at[1])

    for half in range(2):
        wait(in1.at[half, pl.ds(0, 7)], send1.at[half])
    wait(in2.at[pl.ds(0, CHIPS - 1)], send2)
    wait(gin1.at[pl.ds(0, CHIPS - 1)], gsend1)
    wait(in3.at[pl.ds(0, 32)], send3.at[0])
    wait(in3.at[pl.ds(0, 31)], send3.at[1])
    wait(in4a.at[pl.ds(0, 7)], send4.at[0])
    wait(in4b.at[pl.ds(0, 7)], send4.at[1])

    @pl.when(me_c == 0)
    def _():
        wait(gin2.at[pl.ds(0, 3)], gsend2)
        wait(half_in, prod_send)

    @pl.when(me_c == 1)
    def _():
        wait(gin2.at[pl.ds(0, 4)], gsend2)

    @pl.when(jnp.logical_and(me_c == 1, me_n // 2 == 0))
    def _():
        wait(dirs_ref, dir_send)
        wait(dirs_ref, dir_send)

    @pl.when(jnp.logical_and(me_c == 1, me_n // 2 == 1))
    def _():
        wait(dirs_ref, dir_send)
        wait(dirs_ref.at[0], dir_send)


def per_device(statistics, gradients, assign, counts):
    blocks = statistics.shape[0]
    vmem = pl.BlockSpec(memory_space=pltpu.VMEM)
    hbm = pl.BlockSpec(memory_space=pltpu.HBM)
    square = (BLOCK, BLOCK)
    shapes = [
        ((blocks * 8, 128), F32),
        ((blocks * 4, 128), BF16),
        ((2, 128), jnp.int32),
        ((1, 128), jnp.int32),
        ((2, 8, 128, 128), BF16),
        ((2, 8, 128, 128), BF16),
        ((2, 1024, 128), F32),
        ((64, 32, 128), BF16),
        ((64, 32, 128), BF16),
        ((512, 128), F32),
        ((1024, 128), F32),
        ((64, 16, 128), BF16),
        ((64, 16, 128), BF16),
        ((1024, 128), F32),
        ((4, 256, 128), BF16),
        ((8, 256, 128), BF16),
        ((4, 512, 128), F32),
        (square, BF16),
        (square, F32),
        (square, F32),
        (square, BF16),
        (square, BF16),
        (square, BF16),
        (square, BF16),
        (square, BF16),
        (square, BF16),
        ((64, 32, 128), BF16),
        ((64, 32, 128), BF16),
        ((2048, 128), F32),
        ((8, 128, 128), BF16),
        ((8, 128, 128), BF16),
        ((8, 144, 128), BF16),
        ((8, 144, 128), BF16),
        ((8, 128, 128), F32),
    ]
    dma = pltpu.SemaphoreType.DMA
    two = dma((2,))
    scratch = [pltpu.VMEM(shape, dtype) for shape, dtype in shapes]
    scratch += [dma((4,)), two, two] + [dma] * 9 + [two] * 5
    roots, diags, dirs = pl.pallas_call(
        kernel,
        out_shape=[
            jax.ShapeDtypeStruct((blocks * 8, 128), F32),
            jax.ShapeDtypeStruct((2, 4, blocks), F32),
            jax.ShapeDtypeStruct((2, BLOCK, BLOCK), BF16),
        ],
        in_specs=[hbm] * 4,
        out_specs=[vmem, vmem, vmem],
        scratch_shapes=scratch,
        compiler_params=pltpu.CompilerParams(
            collective_id=0, has_side_effects=True, vmem_limit_bytes=40 * 2**20
        ),
        cost_estimate=pl.CostEstimate(
            flops=2 * 6 * BLOCK**3, bytes_accessed=4 * 2**20, transcendentals=0
        ),
        name="shampoo_roots",
    )(
        statistics.reshape(blocks * 8, 128),
        gradients.reshape(blocks * 4, 128),
        assign.T,
        counts.reshape(1, -1),
    )
    inverse_roots = roots.reshape(statistics.shape)
    root_diagonals = jnp.transpose(diags, (2, 0, 1))
    return inverse_roots, root_diagonals, dirs[None]


def solution(mesh):
    return jax.shard_map(
        per_device,
        mesh=mesh,
        in_specs=(P(None, None, "wide", "narrow"), P(None, "wide", "narrow"), P(), P()),
        out_specs=(
            P(None, None, "wide", "narrow"),
            P(None, None, "wide"),
            P("wide", None, None, None),
        ),
        check_vma=False,
    )
```

time: 91.8 us -> 71.8 us (0.78)
  the two profiles are of different devices: /device:TPU:1 before, /device:TPU:40 now
where the time goes in v2:
time: 71.8 us; the launch traced here: 71.6 us
  Pallas kernels  66 us (92%)
  local copies, waits for them, and re-layouts  4.97 us (7%)
    pallas_call x1, Pallas kernels, per_device(): pl.pallas_call(kernel, out_shape=[jax.ShapeDtypeStruct((blocks * 8, 128),...  66 us
    unnamed x11, local copies, waits for them, and re-layouts  4.97 us

profile of v2, /device:TPU:40, one launch (start us, length us, event | category | flops | bytes accessed | tf_op | source)
XLA Modules:
  0.0 71.6 jit_solution(10178620406454602431)
XLA Ops:
  0.6 0.0 copy-start.2
  0.6 0.0 copy-start.3
  0.7 0.7 copy-done.2
  1.3 0.0 copy-done.3
  1.3 0.0 copy-start
  1.3 1.0 %copy-done = f32[128,2,4,128]{3,2,1,0:T(4,128)S(1)} copy-done((f32[128,2,4,128]{3,2,1,0:T(4,128)S(1)}, f32[128,2,4,128]{3,2,1,0:T(4,128)}, u32[]{:S(2)}) %copy-start) | copy-done | bytes 524312
  2.4 0.0 copy-start.1
  2.4 0.9 %copy-done.1 = bf16[128,4,128]{2,1,0:T(4,128)(2,1)S(1)} copy-done((bf16[128,4,128]{2,1,0:T(4,128)(2,1)S(1)}, bf16[128,4,128]{2,1,0:T(4,128)(2,1)}, u32[]{:S(2)}) %copy-start.1) | copy-done | bytes 131096
  3.3 66.0 %shampoo_roots.1 = (f32[1024,128]{1,0:T(8,128)S(1)}, f32[2,4,128]{2,1,0:T(4,128)S(1)}, bf16[2,512,512]{2,1,0:T(8,128)(2,1)S(1)}) custom-call(f32[1024,128]{1,0:T(8,128)S(1)} %bitcast.10, bf16[512,128]{1,0:T(8,128)(2,1)S(1)} %bitcast.11, s32[2,128]{1,0:T(2,128)S(1)} %bitcast.12, s32[1,128]{1,0:T(1,128)S(1)} %bitcast.13), custom_call_target="tpu_custom_call" | custom-call | flops 1610612736 | bytes 4194304 | tf_op jit(solution)/shard_map/shampoo_roots/pallas_call | solution.py:487
  69.3 0.8 %copy.10 = f32[128,2,4,128]{3,2,1,0:T(4,128)} copy(f32[128,2,4,128]{3,2,1,0:T(4,128)S(1)} %bitcast.8) | data formatting | bytes 1048576
  70.1 0.6 copy.11
  70.7 1.0 %copy.12 = bf16[1,2,512,512]{3,2,1,0:T(8,128)(2,1)} copy(bf16[1,2,512,512]{3,2,1,0:T(8,128)(2,1)S(1)} %bitcast.7) | data formatting | bytes 2097152
Async XLA Ops:
  0.6 0.7 copy-start.2
  0.6 0.7 copy-start.3
  1.3 1.0 %copy-start = (f32[128,2,4,128]{3,2,1,0:T(4,128)S(1)}, f32[128,2,4,128]{3,2,1,0:T(4,128)}, u32[]{:S(2)}) copy-start(f32[128,2,4,128]{3,2,1,0:T(4,128)} %param.4) | copy-start | bytes 1572868
  2.4 0.9 %copy-start.1 = (bf16[128,4,128]{2,1,0:T(4,128)(2,1)S(1)}, bf16[128,4,128]{2,1,0:T(4,128)(2,1)}, u32[]{:S(2)}) copy-start(bf16[128,4,128]{2,1,0:T(4,128)(2,1)} %param.5) | copy-start | bytes 393220

commit v3 on v2

--- a/solution.py
+++ b/solution.py
@@ -11,19 +11,22 @@
 F32 = jnp.float32
 BF16 = jnp.bfloat16
 
-OWN = 48
-
-
-def steps(place):
-    return place % 8, (place // 8 + 2) % 8
-
-
-def distance(place):
-    return sum(min(s, 8 - s) for s in steps(place))
-
-
-FAR = sorted(range(32), key=lambda p: -distance(p))
-NEAR = sorted((p for p in range(32, 64) if p != OWN), key=lambda p: -distance(p))
+
+def far_first():
+    sizes = [(a, b) for a in range(5) for b in range(5)]
+    sizes.sort(key=lambda s: (-(s[0] + s[1]), abs(s[0] - s[1])))
+    order = []
+    for a, b in sizes:
+        for step in ((a, b), (-a, -b), (a, -b), (-a, b)):
+            step = (step[0] % 8, step[1] % 8)
+            if step not in order:
+                order.append(step)
+    return order
+
+
+STEPS = far_first()
+OWN = CHIPS - 1
+HALVES = (range(32), range(32, OWN))
 
 
 def dot(first, second):
@@ -93,14 +96,18 @@
     half_out,
     half_in,
     dir_out,
+    spread3,
     out3,
     in3,
     flat3,
-    out4a,
-    in4a,
-    out4b,
-    in4b,
+    out4,
+    in4,
+    flat4,
     partial,
+    diag_rows,
+    diag_far,
+    diag_out,
+    diag_in,
     load_sem,
     send1,
     recv1,
@@ -118,6 +125,10 @@
     recv3,
     send4,
     recv4,
+    far_send,
+    far_recv,
+    diag_send,
+    diag_recv,
 ):
     loads = [
         pltpu.make_async_copy(src, dst, load_sem.at[i])
@@ -143,7 +154,7 @@
     along_z = [(me_z + s) % 8 * 8 for s in range(8)]
 
     def chip(place):
-        y, z = steps(place)
+        y, z = STEPS[place]
         return along_z[z] + along_y[y]
 
     def group_mate(i):
@@ -154,20 +165,26 @@
     for i in range(1, 8):
         _, w, n = group_mate(i)
         pl.semaphore_signal(barrier, inc=1, device_id=(w, n), device_id_type=MESH)
-    for place in FAR + NEAR:
+    for place in range(OWN):
         pl.semaphore_signal(
             barrier, inc=1, device_id=(chip(place) * 2 + me_c, me_n), device_id_type=MESH
         )
 
-    def chips_at(shape, axis, sign):
-        place = iota(shape, axis)
-        y, z = place % 8, (place // 8 + 2) % 8
-        return (me_z + sign * z + 8) % 8 * 8 + (me_y + sign * y + 8) % 8
-
+    def steps_column(which):
+        tiles = []
+        for start in range(0, CHIPS, 8):
+            tile = jnp.full((8, 128), STEPS[start][which], jnp.int32)
+            for i in range(1, 8):
+                tile = jnp.where(iota((8, 128), 0) == i, STEPS[start + i][which], tile)
+            tiles.append(tile)
+        return jnp.concatenate(tiles, axis=0)
+
+    step_y, step_z = steps_column(0), steps_column(1)
+    to_worker = 2 * ((me_z + step_z) % 8 * 8 + (me_y + step_y) % 8)
+    from_worker = 2 * ((me_z - step_z + 8) % 8 * 8 + (me_y - step_y + 8) % 8)
+    worker = iota((CHIPS, 128), 1)
     loads[0].wait()
     loads[1].wait()
-    to_worker = 2 * chips_at((CHIPS, 128), 0, 1)
-    from_worker = 2 * chips_at((128, CHIPS), 1, -1)
     listed = []
     taken = []
     for slot in range(2):
@@ -178,10 +195,8 @@
     selects = []
     for m in range(4):
         par, slot = m // 2, m % 2
-        pick = hot(iota((CHIPS, 128), 1) == to_worker + par)
-        gathers.append(dot_nt(pick, listed[slot]).astype(BF16))
-        place = hot(iota((128, CHIPS), 0) == from_worker + par)
-        selects.append(dot(taken[slot], place).astype(BF16))
+        gathers.append(dot_nt(hot(worker == to_worker + par), listed[slot]).astype(BF16))
+        selects.append(dot_nt(taken[slot], hot(worker == from_worker + par)).astype(BF16))
     gather = jnp.concatenate(gathers, axis=0)
 
     loads[2].wait()
@@ -216,12 +231,12 @@
             send(
                 out1.at[half, g], in1.at[half, me_g], send1.at[half], recv1.at[half], w, n
             )
-    for place in FAR + NEAR:
+    for place in range(OWN):
         send(
             gout1.at[place], gin1.at[me_j], gsend1, grecv1, chip(place) * 2 + me_c, me_n
         )
 
-    for half, places in enumerate((FAR, NEAR)):
+    for half, places in enumerate(HALVES):
         wait(in1.at[half, pl.ds(0, 7)], recv1.at[half])
         flat1[half] = in1[half].reshape(1024, 128).astype(F32)
         if half == 1:
@@ -279,24 +294,37 @@
     root = scale4 * (jnp.where(eye, 25.0, 0.0) + tail)
     work[...] = root
     low_root[...] = root.astype(BF16)
-
-    def rows_for(place):
-        rows = pl.ds(pl.multiple_of(chip(place) * 8, 8), 8)
-        parts = [work[rows, 128 * n : 128 * n + 128] for n in range(4)]
-        return jnp.concatenate(parts, axis=0).astype(BF16)
-
-    for half, places in enumerate((FAR, NEAR)):
-        for place in places:
-            out3[place] = rows_for(place)
+    diagonal = jnp.sum(jnp.where(eye, root, 0.0), axis=0, keepdims=True)
+    for n in range(4):
+        diag_rows[n] = diagonal[:, 128 * n : 128 * n + 128]
+
+    for half, places in enumerate((range(32), range(32, CHIPS))):
+        for i, place in enumerate(places):
+            rows = pl.ds(pl.multiple_of(chip(place) * 8, 8), 8)
+            for n in range(4):
+                spread3[n, i * 8 : i * 8 + 8, :] = work[rows, 128 * n : 128 * n + 128]
+        for q in range(32):
+            n, core, r = q // 8, q // 4 % 2, q % 4
+            out3[half, n * 2 + core, r * 32 : r * 32 + 32, :] = spread3[
+                n, pl.ds(core * 4 + r, 32, stride=8), :
+            ].astype(BF16)
+        in3[half, me_g] = out3[half, me_g]
+        for i in (4, 5, 3, 2, 6, 7, 1):
+            g, w, n = group_mate(i)
             send(
-                out3.at[place],
-                in3.at[place],
-                send3.at[half],
-                recv3.at[half],
-                chip(place) * 2 + me_c,
-                me_n,
+                out3.at[half, g], in3.at[half, me_g], send3.at[half], recv3.at[half], w, n
             )
-    in3[OWN] = rows_for(OWN)
+
+    for place in range(OWN):
+        send(
+            diag_rows.at[chip(place) // 16],
+            diag_far.at[place],
+            far_send,
+            far_recv,
+            chip(place) * 2 + me_c,
+            me_n,
+        )
+    diag_far[OWN] = diag_rows[me_j // 16]
 
     @pl.when(me_c == 0)
     def _():
@@ -344,58 +372,59 @@
     def _():
         dirs_ref[me_n % 2] = dir_out[...]
 
-    wait(in3.at[pl.ds(0, 32)], recv3.at[0])
-    flat3[:1024] = in3[:32].reshape(1024, 128).astype(F32)
-    for q in range(32):
-        out4a[q // 4, q % 4 * 32 : q % 4 * 32 + 32, :] = flat3[pl.ds(q, 32, stride=32), :].astype(
-            BF16
-        )
-    in4a[me_g] = out4a[me_g]
+    for half, places in enumerate(HALVES):
+        wait(in3.at[half, pl.ds(0, 7)], recv3.at[half])
+        flat3[half] = in3[half].reshape(1024, 128).astype(F32)
+        for place in places:
+            out4[place] = flat3[half, pl.ds(place % 32, 32, stride=32), :].astype(BF16)
+            send(
+                out4.at[place],
+                in4.at[place],
+                send4,
+                recv4.at[half],
+                chip(place) * 2 + me_c,
+                me_n,
+            )
+        if half == 1:
+            in4[OWN] = flat3[half, pl.ds(OWN % 32, 32, stride=32), :].astype(BF16)
+
+    wait(diag_far.at[pl.ds(0, OWN)], far_recv)
+    mine = jnp.logical_and(
+        iota((16, 128), 0) < 8, iota((16, 128), 1) == 8 * (me_j % 16) + iota((16, 128), 0)
+    )
+    far = diag_far[...].reshape(CHIPS, 128).astype(BF16)
+    diag_out[...] = jnp.concatenate(
+        [dot_nt(hot(mine), far), jnp.zeros((16, CHIPS), F32)], axis=1
+    ).astype(BF16)
+    diag_in[me_g] = diag_out[...]
     for i in (4, 5, 3, 2, 6, 7, 1):
         g, w, n = group_mate(i)
-        send(out4a.at[g], in4a.at[me_g], send4.at[0], recv4.at[0], w, n)
-
-    wait(in3.at[pl.ds(0, 31)], recv3.at[1])
-    flat3[1024:] = in3[32:].reshape(1024, 128).astype(F32)
-    for q in range(32):
-        out4b[q // 4, q % 4 * 32 : q % 4 * 32 + 32, :] = flat3[
-            pl.ds(1024 + q, 32, stride=32), :
-        ].astype(BF16)
-    for core in range(2):
-        diag = jnp.zeros((16, CHIPS), F32)
-        for r in range(4):
-            rows = flat3[pl.ds((me_j // 16) * 8 + core * 4 + r, CHIPS, stride=32), :].astype(BF16)
-            place = jnp.logical_and(
-                iota((16, 128), 0) == r, iota((16, 128), 1) == (8 * me_j + 4 * core + r) % 128
-            )
-            diag = diag + dot_nt(hot(place), rows)
-        padded = jnp.concatenate([diag, jnp.zeros((16, CHIPS), F32)], axis=1).astype(BF16)
-        for n in range(4):
-            out4b[n * 2 + core, 128:144, :] = padded
-    in4b[me_g] = out4b[me_g]
-    for i in (4, 5, 3, 2, 6, 7, 1):
-        g, w, n = group_mate(i)
-        send(out4b.at[g], in4b.at[me_g], send4.at[1], recv4.at[1], w, n)
-
-    def picked_rows(received, k, r, half):
+        send(diag_out, diag_in.at[me_g], diag_send, diag_recv, w, n)
+
+    def picked_rows(k, r, half):
         select = jnp.concatenate([s[:, half * 32 : half * 32 + 32] for s in selects], axis=1)
-        rows = [received[m * 2 + k, r * 32 : r * 32 + 32, :] for m in range(4)]
+        starts = [half * 1024 + (m * 2 + k) * 4 + r for m in range(4)]
+        rows = [flat4[pl.ds(start, 32, stride=32), :].astype(BF16) for start in starts]
         return dot(select, jnp.concatenate(rows, axis=0))
 
-    wait(in4a.at[pl.ds(0, 7)], recv4.at[0])
+    wait(in4.at[pl.ds(0, 32)], recv4.at[0])
+    flat4[:1024] = in4[:32].reshape(1024, 128).astype(F32)
     for k in range(2):
         for r in range(4):
-            partial[k * 4 + r] = picked_rows(in4a, k, r, 0)
-    wait(in4b.at[pl.ds(0, 7)], recv4.at[1])
+            partial[k * 4 + r] = picked_rows(k, r, 0)
+    wait(diag_in.at[pl.ds(0, 7)], diag_recv)
+    for k in range(2):
+        diag = jnp.zeros((16, 128), F32)
+        for m in range(4):
+            diag = diag + dot_nt(diag_in[m * 2 + k][:, :CHIPS], selects[m])
+        diag_ref[k] = jnp.where(me_c == 0, diag[0:4], diag[4:8])
+    wait(in4.at[pl.ds(0, 31)], recv4.at[1])
+    flat4[1024:] = in4[32:].reshape(1024, 128).astype(F32)
     for k in range(2):
         for r in range(4):
-            full = partial[k * 4 + r] + picked_rows(in4b, k, r, 1)
+            full = partial[k * 4 + r] + picked_rows(k, r, 1)
             on_diag = iota((128, 128), 1) + 128 * me_n == 4 * wide + r
             roots_ref[pl.ds(k * 4 + r, 128, stride=8), :] = jnp.where(on_diag, 0.0, full)
-        diag = jnp.zeros((16, 128), F32)
-        for m in range(4):
-            diag = diag + dot_nt(in4b[m * 2 + k, 128:144, :][:, :CHIPS], selects[m])
-        diag_ref[k] = diag[:4]
 
     @pl.when(jnp.logical_and(me_c == 1, me_n == 2))
     def _():
@@ -414,10 +443,11 @@
         wait(in1.at[half, pl.ds(0, 7)], send1.at[half])
     wait(in2.at[pl.ds(0, CHIPS - 1)], send2)
     wait(gin1.at[pl.ds(0, CHIPS - 1)], gsend1)
-    wait(in3.at[pl.ds(0, 32)], send3.at[0])
-    wait(in3.at[pl.ds(0, 31)], send3.at[1])
-    wait(in4a.at[pl.ds(0, 7)], send4.at[0])
-    wait(in4b.at[pl.ds(0, 7)], send4.at[1])
+    for half in range(2):
+        wait(in3.at[half, pl.ds(0, 7)], send3.at[half])
+    wait(in4.at[pl.ds(0, CHIPS - 1)], send4)
+    wait(diag_far.at[pl.ds(0, OWN)], far_send)
+    wait(diag_in.at[pl.ds(0, 7)], diag_send)
 
     @pl.when(me_c == 0)
     def _():
@@ -471,19 +501,23 @@
         (square, BF16),
         (square, BF16),
         (square, BF16),
+        ((4, 256, 128), F32),
+        ((2, 8, 128, 128), BF16),
+        ((2, 8, 128, 128), BF16),
+        ((2, 1024, 128), F32),
         ((64, 32, 128), BF16),
         ((64, 32, 128), BF16),
         ((2048, 128), F32),
-        ((8, 128, 128), BF16),
-        ((8, 128, 128), BF16),
-        ((8, 144, 128), BF16),
-        ((8, 144, 128), BF16),
         ((8, 128, 128), F32),
+        ((4, 1, 128), F32),
+        ((64, 1, 128), F32),
+        ((16, 128), BF16),
+        ((8, 16, 128), BF16),
     ]
     dma = pltpu.SemaphoreType.DMA
     two = dma((2,))
     scratch = [pltpu.VMEM(shape, dtype) for shape, dtype in shapes]
-    scratch += [dma((4,)), two, two] + [dma] * 9 + [two] * 5
+    scratch += [dma((4,)), two, two] + [dma] * 9 + [two] * 3 + [dma, two] + [dma] * 4
     roots, diags, dirs = pl.pallas_call(
         kernel,
         out_shape=[

time: 71.8 us -> 68.9 us (0.960)
  the two profiles are of different devices: /device:TPU:40 before, /device:TPU:1 now
where the time goes in v3:
time: 68.9 us; the launch traced here: 68 us
  Pallas kernels  62.3 us (90%)
  local copies, waits for them, and re-layouts  4.97 us (7%)
    pallas_call x1, Pallas kernels, per_device(): pl.pallas_call(kernel, out_shape=[jax.ShapeDtypeStruct((blocks * 8, 128),...  62.3 us
    unnamed x11, local copies, waits for them, and re-layouts  4.97 us

profile of v3, /device:TPU:1, one launch (start us, length us, event | category | flops | bytes accessed | tf_op | source)
XLA Modules:
  0.0 68.0 jit_solution(4731929417127574282)
XLA Ops:
  0.6 0.0 copy-start.2
  0.6 0.0 copy-start.3
  0.7 0.7 copy-done.2
  1.3 0.0 copy-done.3
  1.3 0.0 copy-start
  1.3 1.0 %copy-done = f32[128,2,4,128]{3,2,1,0:T(4,128)S(1)} copy-done((f32[128,2,4,128]{3,2,1,0:T(4,128)S(1)}, f32[128,2,4,128]{3,2,1,0:T(4,128)}, u32[]{:S(2)}) %copy-start) | copy-done | bytes 524312
  2.4 0.0 copy-start.1
  2.4 0.9 %copy-done.1 = bf16[128,4,128]{2,1,0:T(4,128)(2,1)S(1)} copy-done((bf16[128,4,128]{2,1,0:T(4,128)(2,1)S(1)}, bf16[128,4,128]{2,1,0:T(4,128)(2,1)}, u32[]{:S(2)}) %copy-start.1) | copy-done | bytes 131096
  3.3 62.3 %shampoo_roots.1 = (f32[1024,128]{1,0:T(8,128)S(1)}, f32[2,4,128]{2,1,0:T(4,128)S(1)}, bf16[2,512,512]{2,1,0:T(8,128)(2,1)S(1)}) custom-call(f32[1024,128]{1,0:T(8,128)S(1)} %bitcast.10, bf16[512,128]{1,0:T(8,128)(2,1)S(1)} %bitcast.11, s32[2,128]{1,0:T(2,128)S(1)} %bitcast.12, s32[1,128]{1,0:T(1,128)S(1)} %bitcast.13), custom_call_target="tpu_custom_call" | custom-call | flops 1610612736 | bytes 4194304 | tf_op jit(solution)/shard_map/shampoo_roots/pallas_call | solution.py:521
  65.6 0.8 %copy.10 = f32[128,2,4,128]{3,2,1,0:T(4,128)} copy(f32[128,2,4,128]{3,2,1,0:T(4,128)S(1)} %bitcast.8) | data formatting | bytes 1048576
  66.4 0.6 copy.11
  67.0 1.0 %copy.12 = bf16[1,2,512,512]{3,2,1,0:T(8,128)(2,1)} copy(bf16[1,2,512,512]{3,2,1,0:T(8,128)(2,1)S(1)} %bitcast.7) | data formatting | bytes 2097152
Async XLA Ops:
  0.6 0.7 %copy-start.2 = (s32[128,2]{0,1:T(2,128)S(1)}, s32[128,2]{0,1:T(2,128)}, u32[]{:S(2)}) copy-start(s32[128,2]{0,1:T(2,128)} %param.6) | copy-start | bytes 3076
  0.6 0.7 copy-start.3
  1.3 1.0 %copy-start = (f32[128,2,4,128]{3,2,1,0:T(4,128)S(1)}, f32[128,2,4,128]{3,2,1,0:T(4,128)}, u32[]{:S(2)}) copy-start(f32[128,2,4,128]{3,2,1,0:T(4,128)} %param.4) | copy-start | bytes 1572868
  2.4 0.9 %copy-start.1 = (bf16[128,4,128]{2,1,0:T(4,128)(2,1)S(1)}, bf16[128,4,128]{2,1,0:T(4,128)(2,1)}, u32[]{:S(2)}) copy-start(bf16[128,4,128]{2,1,0:T(4,128)(2,1)} %param.5) | copy-start | bytes 393220

commit v4 on v3

--- a/solution.py
+++ b/solution.py
@@ -104,10 +104,11 @@
     in4,
     flat4,
     partial,
-    diag_rows,
-    diag_far,
+    diag_pick,
     diag_out,
     diag_in,
+    diag_out2,
+    diag_in2,
     load_sem,
     send1,
     recv1,
@@ -125,10 +126,10 @@
     recv3,
     send4,
     recv4,
-    far_send,
-    far_recv,
     diag_send,
     diag_recv,
+    diag_send2,
+    diag_recv2,
 ):
     loads = [
         pltpu.make_async_copy(src, dst, load_sem.at[i])
@@ -183,6 +184,9 @@
     to_worker = 2 * ((me_z + step_z) % 8 * 8 + (me_y + step_y) % 8)
     from_worker = 2 * ((me_z - step_z + 8) % 8 * 8 + (me_y - step_y + 8) % 8)
     worker = iota((CHIPS, 128), 1)
+    for n in range(4):
+        columns = iota((CHIPS, 128), 1) + 128 * n
+        diag_pick[:, 128 * n : 128 * n + 128] = hot(columns // 8 * 2 == to_worker)
     loads[0].wait()
     loads[1].wait()
     listed = []
@@ -295,9 +299,15 @@
     work[...] = root
     low_root[...] = root.astype(BF16)
     diagonal = jnp.sum(jnp.where(eye, root, 0.0), axis=0, keepdims=True)
-    for n in range(4):
-        diag_rows[n] = diagonal[:, 128 * n : 128 * n + 128]
-
+    spread = jnp.where(iota((16, BLOCK), 1) % 8 == iota((16, BLOCK), 0), diagonal, 0.0)
+    diag_out[...] = jnp.concatenate(
+        [dot_nt(spread.astype(BF16), diag_pick[...]), jnp.zeros((16, CHIPS), F32)], axis=1
+    ).astype(BF16)
+    diag_in[me_g] = diag_out[...]
+
+    for i in (4, 5, 3, 2, 6, 7, 1):
+        g, w, n = group_mate(i)
+        send(diag_out, diag_in.at[me_g], diag_send, diag_recv, w, n)
     for half, places in enumerate((range(32), range(32, CHIPS))):
         for i, place in enumerate(places):
             rows = pl.ds(pl.multiple_of(chip(place) * 8, 8), 8)
@@ -315,17 +325,6 @@
                 out3.at[half, g], in3.at[half, me_g], send3.at[half], recv3.at[half], w, n
             )
 
-    for place in range(OWN):
-        send(
-            diag_rows.at[chip(place) // 16],
-            diag_far.at[place],
-            far_send,
-            far_recv,
-            chip(place) * 2 + me_c,
-            me_n,
-        )
-    diag_far[OWN] = diag_rows[me_j // 16]
-
     @pl.when(me_c == 0)
     def _():
         wait(gin2.at[pl.ds(0, 7)], grecv2)
@@ -339,40 +338,63 @@
         half_out[...] = dot(low_root[...], grad[...]).astype(BF16)
         send(half_out, half_in, prod_send, prod_recv, me_j * 2 + 1, me_n)
 
-    @pl.when(me_c == 1)
-    def _():
-        mine = jnp.logical_and(
-            iota((1, 128), 1) == 2 * me_j + me_n // 2, counts_ref[...] > me_n % 2
-        )
-        keep = jnp.sum(jnp.where(mine, 1.0, 0.0), axis=1, keepdims=True)
-        wait(half_in, prod_recv)
-        dir_out[...] = (dot(half_in[...], low_root[...]) * keep).astype(BF16)
-        for d in (2, 1, 3):
+    def send_diagonals():
+        wait(diag_in.at[pl.ds(0, 7)], diag_recv)
+        tiles = []
+        for g in range(8):
+            tile = diag_in[g].astype(F32)
+            tiles.append(jnp.where(me_c == 0, tile[0:4], tile[4:8]))
+        tiles.append(jnp.zeros((96, 128), F32))
+        diag_out2[...] = jnp.concatenate(tiles, axis=0).T[:CHIPS].reshape(CHIPS, 1, 128)
+        for place in range(OWN):
+            send(
+                diag_out2.at[place],
+                diag_in2.at[place],
+                diag_send2,
+                diag_recv2,
+                chip(place) * 2 + me_c,
+                me_n,
+            )
+        diag_in2[OWN] = diag_out2[OWN]
+
+    def send_directions():
+        @pl.when(me_c == 1)
+        def _():
+            mine = jnp.logical_and(
+                iota((1, 128), 1) == 2 * me_j + me_n // 2, counts_ref[...] > me_n % 2
+            )
+            keep = jnp.sum(jnp.where(mine, 1.0, 0.0), axis=1, keepdims=True)
+            wait(half_in, prod_recv)
+            dir_out[...] = (dot(half_in[...], low_root[...]) * keep).astype(BF16)
+            for d in (2, 1, 3):
+                send(
+                    dir_out,
+                    dirs_ref.at[me_n % 2],
+                    dir_send,
+                    dir_recv.at[me_n % 2],
+                    me_j * 2 + me_n // 2,
+                    (me_n + d) % 4,
+                )
+
+        @pl.when(jnp.logical_and(me_c == 1, me_n // 2 == 0))
+        def _():
             send(
                 dir_out,
                 dirs_ref.at[me_n % 2],
                 dir_send,
                 dir_recv.at[me_n % 2],
-                me_j * 2 + me_n // 2,
-                (me_n + d) % 4,
-            )
-
-    @pl.when(jnp.logical_and(me_c == 1, me_n // 2 == 0))
-    def _():
-        send(
-            dir_out,
-            dirs_ref.at[me_n % 2],
-            dir_send,
-            dir_recv.at[me_n % 2],
-            me_j * 2,
-            me_n,
-        )
-
-    @pl.when(jnp.logical_and(me_c == 1, me_n // 2 == 1))
-    def _():
-        dirs_ref[me_n % 2] = dir_out[...]
+                me_j * 2,
+                me_n,
+            )
+
+        @pl.when(jnp.logical_and(me_c == 1, me_n // 2 == 1))
+        def _():
+            dirs_ref[me_n % 2] = dir_out[...]
 
     for half, places in enumerate(HALVES):
+        if half == 1:
+            send_diagonals()
+            send_directions()
         wait(in3.at[half, pl.ds(0, 7)], recv3.at[half])
         flat3[half] = in3[half].reshape(1024, 128).astype(F32)
         for place in places:
@@ -388,19 +410,6 @@
         if half == 1:
             in4[OWN] = flat3[half, pl.ds(OWN % 32, 32, stride=32), :].astype(BF16)
 
-    wait(diag_far.at[pl.ds(0, OWN)], far_recv)
-    mine = jnp.logical_and(
-        iota((16, 128), 0) < 8, iota((16, 128), 1) == 8 * (me_j % 16) + iota((16, 128), 0)
-    )
-    far = diag_far[...].reshape(CHIPS, 128).astype(BF16)
-    diag_out[...] = jnp.concatenate(
-        [dot_nt(hot(mine), far), jnp.zeros((16, CHIPS), F32)], axis=1
-    ).astype(BF16)
-    diag_in[me_g] = diag_out[...]
-    for i in (4, 5, 3, 2, 6, 7, 1):
-        g, w, n = group_mate(i)
-        send(diag_out, diag_in.at[me_g], diag_send, diag_recv, w, n)
-
     def picked_rows(k, r, half):
         select = jnp.concatenate([s[:, half * 32 : half * 32 + 32] for s in selects], axis=1)
         starts = [half * 1024 + (m * 2 + k) * 4 + r for m in range(4)]
@@ -412,12 +421,13 @@
     for k in range(2):
         for r in range(4):
             partial[k * 4 + r] = picked_rows(k, r, 0)
-    wait(diag_in.at[pl.ds(0, 7)], diag_recv)
+    wait(diag_in2.at[pl.ds(0, OWN)], diag_recv2)
+    by_slot = diag_in2[...].reshape(CHIPS, 128).T[:32].astype(BF16)
+    diag = jnp.zeros((8, 128), F32)
+    for m in range(4):
+        diag = diag + dot_nt(by_slot, selects[m])[8 * m : 8 * m + 8]
     for k in range(2):
-        diag = jnp.zeros((16, 128), F32)
-        for m in range(4):
-            diag = diag + dot_nt(diag_in[m * 2 + k][:, :CHIPS], selects[m])
-        diag_ref[k] = jnp.where(me_c == 0, diag[0:4], diag[4:8])
+        diag_ref[k] = diag[4 * k : 4 * k + 4]
     wait(in4.at[pl.ds(0, 31)], recv4.at[1])
     flat4[1024:] = in4[32:].reshape(1024, 128).astype(F32)
     for k in range(2):
@@ -446,8 +456,8 @@
     for half in range(2):
         wait(in3.at[half, pl.ds(0, 7)], send3.at[half])
     wait(in4.at[pl.ds(0, CHIPS - 1)], send4)
-    wait(diag_far.at[pl.ds(0, OWN)], far_send)
     wait(diag_in.at[pl.ds(0, 7)], diag_send)
+    wait(diag_in2.at[pl.ds(0, OWN)], diag_send2)
 
     @pl.when(me_c == 0)
     def _():
@@ -509,10 +519,11 @@
         ((64, 32, 128), BF16),
         ((2048, 128), F32),
         ((8, 128, 128), F32),
-        ((4, 1, 128), F32),
-        ((64, 1, 128), F32),
+        ((64, BLOCK), BF16),
         ((16, 128), BF16),
         ((8, 16, 128), BF16),
+        ((64, 1, 128), F32),
+        ((64, 1, 128), F32),
     ]
     dma = pltpu.SemaphoreType.DMA
     two = dma((2,))
@@ -536,10 +547,15 @@
         ),
         name="shampoo_roots",
     )(
-        statistics.reshape(blocks * 8, 128),
-        gradients.reshape(blocks * 4, 128),
-        assign.T,
-        counts.reshape(1, -1),
+        *(
+            pltpu.with_memory_space_constraint(x, pltpu.HBM)
+            for x in (
+                statistics.reshape(blocks * 8, 128),
+                gradients.reshape(blocks * 4, 128),
+                assign.T,
+                counts.reshape(1, -1),
+            )
+        ),
     )
     inverse_roots = roots.reshape(statistics.shape)
     root_diagonals = jnp.transpose(diags, (2, 0, 1))

time: 68.9 us -> 66.1 us (0.959); the launches traced: 68 us -> 66 us
  local copies, waits for them, and re-layouts: 4.97 us -> 2.36 us
  Pallas kernels: 62.3 us -> 63 us
    unnamed x11 -> x3, local copies, waits for them, and re-layouts: 4.97 us -> 2.36 us
where the time goes in v4:
time: 66.1 us; the launch traced here: 66 us
  Pallas kernels  63 us (95%)
  local copies, waits for them, and re-layouts  2.36 us (4%)
    pallas_call x1, Pallas kernels, per_device(): pl.pallas_call(kernel, out_shape=[jax.ShapeDtypeStruct((blocks * 8, 128),...  63 us
    unnamed x3, local copies, waits for them, and re-layouts  2.36 us

profile of v4, /device:TPU:1, one launch (start us, length us, event | category | flops | bytes accessed | tf_op | source)
XLA Modules:
  0.0 66.0 jit_solution(262667048454838525)
XLA Ops:
  0.6 63.0 %shampoo_roots.1 = (f32[1024,128]{1,0:T(8,128)S(1)}, f32[2,4,128]{2,1,0:T(4,128)S(1)}, bf16[2,512,512]{2,1,0:T(8,128)(2,1)S(1)}) custom-call(f32[1024,128]{1,0:T(8,128)} %bitcast.10, bf16[512,128]{1,0:T(8,128)(2,1)} %bitcast.11, s32[2,128]{1,0:T(2,128)} %bitcast.12, s32[1,128]{1,0:T(1,128)} %bitcast.13), custom_call_target="tpu_custom_call" | custom-call | flops 1610612736 | bytes 4194304 | tf_op jit(solution)/shard_map/shampoo_roots/pallas_call | solution.py:532
  63.6 0.8 %copy.10 = f32[128,2,4,128]{3,2,1,0:T(4,128)} copy(f32[128,2,4,128]{3,2,1,0:T(4,128)S(1)} %bitcast.8) | data formatting | bytes 1048576
  64.4 0.6 copy.11
  65.0 1.0 %copy.12 = bf16[1,2,512,512]{3,2,1,0:T(8,128)(2,1)} copy(bf16[1,2,512,512]{3,2,1,0:T(8,128)(2,1)S(1)} %bitcast.7) | data formatting | bytes 2097152

commit v5 on v4

--- a/solution.py
+++ b/solution.py
@@ -14,7 +14,7 @@
 
 def far_first():
     sizes = [(a, b) for a in range(5) for b in range(5)]
-    sizes.sort(key=lambda s: (-(s[0] + s[1]), abs(s[0] - s[1])))
+    sizes.sort(key=lambda s: (-max(s), -(s[0] + s[1])))
     order = []
     for a, b in sizes:
         for step in ((a, b), (-a, -b), (a, -b), (-a, b)):
@@ -217,6 +217,15 @@
                     out1[half, m * 2 + k, r * 32 : r * 32 + 32, :] = picked[start : start + 32]
     for half in range(2):
         in1[half, me_g] = out1[half, me_g]
+
+    pl.semaphore_wait(barrier, 70)
+
+    for half in range(2):
+        for i in (4, 5, 3, 2, 6, 7, 1):
+            g, w, n = group_mate(i)
+            send(
+                out1.at[half, g], in1.at[half, me_g], send1.at[half], recv1.at[half], w, n
+            )
     loads[3].wait()
     gflat[...] = grad_ref[...].astype(F32)
     for r in range(4):
@@ -226,15 +235,6 @@
             gspread[pl.ds(m * 4 + r, 64, stride=16), :] = picked[m * 64 : m * 64 + 64]
     gout1[...] = gspread[...].reshape(CHIPS, 16, 128).astype(BF16)
     gin1[me_j] = gout1[OWN]
-
-    pl.semaphore_wait(barrier, 70)
-
-    for half in range(2):
-        for i in (4, 5, 3, 2, 6, 7, 1):
-            g, w, n = group_mate(i)
-            send(
-                out1.at[half, g], in1.at[half, me_g], send1.at[half], recv1.at[half], w, n
-            )
     for place in range(OWN):
         send(
             gout1.at[place], gin1.at[me_j], gsend1, grecv1, chip(place) * 2 + me_c, me_n
@@ -298,16 +298,7 @@
     root = scale4 * (jnp.where(eye, 25.0, 0.0) + tail)
     work[...] = root
     low_root[...] = root.astype(BF16)
-    diagonal = jnp.sum(jnp.where(eye, root, 0.0), axis=0, keepdims=True)
-    spread = jnp.where(iota((16, BLOCK), 1) % 8 == iota((16, BLOCK), 0), diagonal, 0.0)
-    diag_out[...] = jnp.concatenate(
-        [dot_nt(spread.astype(BF16), diag_pick[...]), jnp.zeros((16, CHIPS), F32)], axis=1
-    ).astype(BF16)
-    diag_in[me_g] = diag_out[...]
-
-    for i in (4, 5, 3, 2, 6, 7, 1):
-        g, w, n = group_mate(i)
-        send(diag_out, diag_in.at[me_g], diag_send, diag_recv, w, n)
+
     for half, places in enumerate((range(32), range(32, CHIPS))):
         for i, place in enumerate(places):
             rows = pl.ds(pl.multiple_of(chip(place) * 8, 8), 8)
@@ -324,6 +315,16 @@
             send(
                 out3.at[half, g], in3.at[half, me_g], send3.at[half], recv3.at[half], w, n
             )
+
+    diagonal = jnp.sum(jnp.where(eye, work[...], 0.0), axis=0, keepdims=True)
+    spread = jnp.where(iota((16, BLOCK), 1) % 8 == iota((16, BLOCK), 0), diagonal, 0.0)
+    diag_out[...] = jnp.concatenate(
+        [dot_nt(spread.astype(BF16), diag_pick[...]), jnp.zeros((16, CHIPS), F32)], axis=1
+    ).astype(BF16)
+    diag_in[me_g] = diag_out[...]
+    for i in (4, 5, 3, 2, 6, 7, 1):
+        g, w, n = group_mate(i)
+        send(diag_out, diag_in.at[me_g], diag_send, diag_recv, w, n)
 
     @pl.when(me_c == 0)
     def _():
@@ -410,11 +411,15 @@
         if half == 1:
             in4[OWN] = flat3[half, pl.ds(OWN % 32, 32, stride=32), :].astype(BF16)
 
+    by_half = [
+        jnp.concatenate([s[:, half * 32 : half * 32 + 32] for s in selects], axis=1)
+        for half in range(2)
+    ]
+
     def picked_rows(k, r, half):
-        select = jnp.concatenate([s[:, half * 32 : half * 32 + 32] for s in selects], axis=1)
         starts = [half * 1024 + (m * 2 + k) * 4 + r for m in range(4)]
         rows = [flat4[pl.ds(start, 32, stride=32), :].astype(BF16) for start in starts]
-        return dot(select, jnp.concatenate(rows, axis=0))
+        return dot(by_half[half], jnp.concatenate(rows, axis=0))
 
     wait(in4.at[pl.ds(0, 32)], recv4.at[0])
     flat4[:1024] = in4[:32].reshape(1024, 128).astype(F32)

time: 66.1 us -> 66.6 us (level)
  no operation moved by 1% of the time
where the time goes in v5:
time: 66.6 us; the launch traced here: 66.5 us
  Pallas kernels  63.5 us (95%)
  local copies, waits for them, and re-layouts  2.36 us (4%)
    pallas_call x1, Pallas kernels, per_device(): pl.pallas_call(kernel, out_shape=[jax.ShapeDtypeStruct((blocks * 8, 128),...  63.5 us
    unnamed x3, local copies, waits for them, and re-layouts  2.36 us

profile of v5, /device:TPU:1, one launch (start us, length us, event | category | flops | bytes accessed | tf_op | source)
XLA Modules:
  0.0 66.5 jit_solution(13746467959722939503)
XLA Ops:
  0.6 63.5 %shampoo_roots.1 = (f32[1024,128]{1,0:T(8,128)S(1)}, f32[2,4,128]{2,1,0:T(4,128)S(1)}, bf16[2,512,512]{2,1,0:T(8,128)(2,1)S(1)}) custom-call(f32[1024,128]{1,0:T(8,128)} %bitcast.10, bf16[512,128]{1,0:T(8,128)(2,1)} %bitcast.11, s32[2,128]{1,0:T(2,128)} %bitcast.12, s32[1,128]{1,0:T(1,128)} %bitcast.13), custom_call_target="tpu_custom_call" | custom-call | flops 1610612736 | bytes 4194304 | tf_op jit(solution)/shard_map/shampoo_roots/pallas_call | solution.py:537
  64.1 0.8 %copy.10 = f32[128,2,4,128]{3,2,1,0:T(4,128)} copy(f32[128,2,4,128]{3,2,1,0:T(4,128)S(1)} %bitcast.8) | data formatting | bytes 1048576
  64.9 0.6 copy.11
  65.5 1.0 %copy.12 = bf16[1,2,512,512]{3,2,1,0:T(8,128)(2,1)} copy(bf16[1,2,512,512]{3,2,1,0:T(8,128)(2,1)S(1)} %bitcast.7) | data formatting | bytes 2097152
